TPU v7x, 32 devices: a whole 2x2x4 slice. The times are simulated.
32 devices in a mesh: grp: 2 (over y), row: 8 (over z, x), col: 2 (over core).
Axes of the slice: x: 2, y: 2, z: 4, core: 2. Of those that a mesh axis runs over, the one named last changes fastest.
Arguments:
- tokens: bfloat16 [128, 256, 180], P(('grp', 'row'), 'col'), parts along dimension 0, may hold values from -6 to 6
- grad_out: bfloat16 [128, 256, 180], P(('grp', 'row'), 'col'), parts along dimension 0, may hold values from -8 to 8
- regions: int32 [128, 256], P(('grp', 'row'), 'col'), parts along dimension 0, may hold values from 0 to 15, as said below
- ln_gain: float32 [180], replicated, may hold values from 0.1 to 1.9
- ln_offset: float32 [180], replicated, may hold values from -1.5 to 1.5
- qkv_weight: bfloat16 [180, 540], replicated, may hold values from -0.4375 to 0.4375
- qkv_bias: float32 [540], replicated, may hold values from -1.5 to 1.5
- proj_weight: bfloat16 [180, 180], replicated, may hold values from -0.4375 to 0.4375
- bias_table: float32 [225, 6], replicated, may hold values from -4 to 320
Outputs:
- d_tokens: bfloat16 [128, 256, 180], P(('grp', 'row'), 'col'), parts along dimension 0
- d_qkv_weight: float32 [360, 540], P('grp'), parts along dimension 0
- d_qkv_bias: float32 [1080], P('grp'), parts along dimension 0
- d_proj_weight: float32 [360, 180], P('grp'), parts along dimension 0
- d_bias_table: float32 [450, 6], P('grp'), parts along dimension 0
- d_ln_gain: float32 [360], P('grp'), parts along dimension 0
- d_ln_offset: float32 [360], P('grp'), parts along dimension 0
There are 2 independent parts, one for each index of `grp`. A program takes and returns all parts, laid end to end along the dimension named above; an argument that names none is the same for every part. Nothing has to cross between parts.
Inputs may be any that keep to these rules, and one draw needn't show every extreme that they name: `regions`: A token attends only to tokens of its window with the same id. The map is a grid: the id is 4 a + b, where a, from 0 to 3, depends only on the token's row and b, from 0 to 3, only on its column.
All inputs are finite; a program needn't handle non-finite values.
Results may differ from a plain program's by a relative error of at most 0.0085.
Values may be sent and summed in bfloat16 or wider, within the bound.
A program may use at most 64 MiB of HBM per device.

v0:
```python
import jax
import jax.numpy as jnp
from jax import lax
from jax.sharding import PartitionSpec as P

HEADS = 6
WIN = 8
SHIFT = 4


masked_score = -10000.0


def from_behind(shard, axis, by):
    count = lax.axis_size(axis)
    return lax.ppermute(shard, axis, [(i, (i + by) % count) for i in range(count)])


def multiply(form, left, right):
    return jnp.einsum(form, left, right, preferred_element_type=jnp.float32)


def relative_onehot(table_rows):
    span_size = WIN * WIN
    position = jnp.arange(span_size, dtype=jnp.int32)
    row_pos = position // WIN
    col_pos = position % WIN
    entry_index = (
        (row_pos[:, None] - row_pos[None, :] + WIN - 1) * (2 * WIN - 1)
        + col_pos[:, None]
        - col_pos[None, :]
        + WIN
        - 1
    )
    return (
        entry_index.reshape(-1)[:, None] == jnp.arange(table_rows, dtype=jnp.int32)[None, :]
    ).astype(jnp.float32)


def normalize(values, gain_vec, offset_vec):
    as_float = values.astype(jnp.float32)
    center = jnp.mean(as_float, -1, keepdims=True)
    variance = jnp.mean(jnp.square(as_float - center), -1, keepdims=True)
    inv_std = lax.rsqrt(variance + 1e-05)
    unit_tokens = (as_float - center) * inv_std
    normed = (unit_tokens * gain_vec + offset_vec).astype(jnp.bfloat16)
    return (normed, unit_tokens, inv_std)


def project(normed, weights, offsets):
    channels = normed.shape[-1]
    summed = multiply("rcd,df->rcf", normed, weights) + offsets
    factor = jnp.where(jnp.arange(3 * channels) < channels, (channels // HEADS) ** (-0.5), 1.0)
    return (summed * factor).astype(jnp.bfloat16)


def window_band(qkv, grad_band, label_band, rel_bias, proj_weight):
    channels = grad_band.shape[-1]
    head_count = rel_bias.shape[0]
    head_size = channels // head_count
    tile_cols = grad_band.shape[1]
    win_count = tile_cols // WIN
    span_size = WIN * WIN

    def windows(array):
        array = array.reshape((WIN, win_count, WIN) + array.shape[2:])
        array = jnp.moveaxis(array, 1, 0)
        return array.reshape((win_count, span_size) + array.shape[3:])

    parted = windows(qkv).reshape(win_count, span_size, 3, head_count, head_size)
    query_part = parted[:, :, 0]
    key_part = parted[:, :, 1]
    value_part = parted[:, :, 2]
    grad_win = windows(grad_band)
    label_win = windows(label_band)
    matched = label_win[:, :, None] == label_win[:, None, :]
    scores = multiply("nihd,njhd->nhij", query_part, key_part) + rel_bias[None]
    scores = jnp.where(matched[:, None], scores, masked_score)
    probability = jax.nn.softmax(scores, axis=-1)
    prob_low = probability.astype(jnp.bfloat16)
    attended = (
        multiply("nhij,njhd->nihd", prob_low, value_part)
        .astype(jnp.bfloat16)
        .reshape(win_count * span_size, channels)
    )
    flat_grad = grad_win.reshape(win_count * span_size, channels)
    d_proj = multiply("tc,td->cd", attended, flat_grad)
    d_attended = (
        multiply("td,cd->tc", flat_grad, proj_weight)
        .astype(jnp.bfloat16)
        .reshape(win_count, span_size, head_count, head_size)
    )
    d_prob = multiply("nihd,njhd->nhij", d_attended, value_part)
    d_scores = probability * (d_prob - jnp.sum(probability * d_prob, -1, keepdims=True))
    score_sum = jnp.sum(d_scores, 0)
    d_score_low = d_scores.astype(jnp.bfloat16)
    d_query = multiply("nhij,njhd->nihd", d_score_low, key_part) * head_size ** (-0.5)
    d_key = multiply("nhij,nihd->njhd", d_score_low, query_part)
    d_value = multiply("nhij,nihd->njhd", prob_low, d_attended)
    d_qkv = (
        jnp.stack([d_query, d_key, d_value], 2)
        .astype(jnp.bfloat16)
        .reshape(win_count, span_size, 3 * channels)
    )
    array = d_qkv
    array = array.reshape((win_count, WIN, WIN) + array.shape[2:])
    array = jnp.moveaxis(array, 0, 1)
    return (array.reshape((WIN, tile_cols) + array.shape[3:]), d_proj, score_sum)


def attention_backward(qkv, grad_tile, label_tile, rel_bias, proj_weight):
    tile_rows = grad_tile.shape[0]
    band_count = tile_rows // WIN
    channels = grad_tile.shape[-1]
    head_count = rel_bias.shape[0]

    def to_bands(array):
        return array.reshape((band_count, WIN) + array.shape[1:])

    def band_step(running, pieces):
        d_qkv, d_proj, score_sum = window_band(
            pieces[0], pieces[1], pieces[2], rel_bias, proj_weight
        )
        return ((running[0] + d_proj, running[1] + score_sum), d_qkv)

    initial = (
        jnp.zeros((channels, channels), jnp.float32),
        jnp.zeros((head_count, WIN * WIN, WIN * WIN), jnp.float32),
    )
    totals, d_qkv = lax.scan(
        band_step, initial, (to_bands(qkv), to_bands(grad_tile), to_bands(label_tile))
    )
    return (d_qkv.reshape((tile_rows,) + d_qkv.shape[2:]), totals[0], totals[1])


def input_backward(d_qkv, normed, unit_tokens, inv_std, gain_vec, qkv_weight):
    d_weight = multiply("rcd,rcf->df", normed, d_qkv)
    d_offsets = jnp.sum(d_qkv.astype(jnp.float32), (0, 1))
    d_normed = multiply("rcf,df->rcd", d_qkv, qkv_weight)
    d_gain = jnp.sum(d_normed * unit_tokens, (0, 1))
    d_offset = jnp.sum(d_normed, (0, 1))
    scaled_grad = d_normed * gain_vec
    d_input = inv_std * (
        scaled_grad
        - jnp.mean(scaled_grad, -1, keepdims=True)
        - unit_tokens * jnp.mean(scaled_grad * unit_tokens, -1, keepdims=True)
    )
    return (d_input, d_weight, d_offsets, d_gain, d_offset)


def into_frame(member_one, member_two, member_three):
    below_one, below_two, below_three = from_behind(
        (member_one[:SHIFT], member_two[:SHIFT], member_three[:SHIFT]), "row", -1
    )
    member_one = jnp.concatenate([member_one[SHIFT:], below_one], 0)
    member_two = jnp.concatenate([member_two[SHIFT:], below_two], 0)
    member_three = jnp.concatenate([member_three[SHIFT:], below_three], 0)
    right_one, right_two, right_three = from_behind(
        (member_one[:, :SHIFT], member_two[:, :SHIFT], member_three[:, :SHIFT]), "col", -1
    )
    member_one = jnp.concatenate([member_one[:, SHIFT:], right_one], 1)
    member_two = jnp.concatenate([member_two[:, SHIFT:], right_two], 1)
    member_three = jnp.concatenate([member_three[:, SHIFT:], right_three], 1)
    return (member_one, member_two, member_three)


def back_proj(field):
    from_left = from_behind(field[:, -SHIFT:], "col", 1)
    field = jnp.concatenate([from_left, field[:, :-SHIFT]], 1)
    from_above = from_behind(field[-SHIFT:], "row", 1)
    return jnp.concatenate([from_above, field[:-SHIFT]], 0)


def table_grad(score_sum, entry_table):
    head_count = score_sum.shape[0]
    flat_sum = jnp.transpose(score_sum, (1, 2, 0)).reshape(-1, head_count)
    return jnp.dot(entry_table.T, flat_sum, precision=lax.Precision.HIGHEST)


def attention_sums(d_proj, d_table):
    return (d_proj, d_table)


def on_device(
    tokens, grad_out, regions, ln_gain, ln_offset, qkv_weight, qkv_bias, proj_weight, bias_table
):
    head_count = bias_table.shape[1]
    entry_table = relative_onehot(bias_table.shape[0])
    rel_bias = (
        jnp.dot(entry_table, bias_table, precision=lax.Precision.HIGHEST)
        .reshape(WIN * WIN, WIN * WIN, head_count)
        .transpose(2, 0, 1)
    )
    labels = regions.astype(jnp.bfloat16)
    normed, unit_tokens, inv_std = normalize(tokens, ln_gain, ln_offset)
    qkv = project(normed, qkv_weight, qkv_bias)
    qkv_framed, grad_framed, label_framed = into_frame(qkv, grad_out, labels)
    d_framed, d_proj, score_sum = attention_backward(
        qkv_framed, grad_framed, label_framed, rel_bias, proj_weight
    )
    d_proj, d_table = attention_sums(d_proj, table_grad(score_sum, entry_table))
    d_qkv = back_proj(d_framed)
    d_input, d_weight, d_offsets, d_gain, d_offset = input_backward(
        d_qkv, normed, unit_tokens, inv_std, ln_gain, qkv_weight
    )
    d_proj, d_table, d_weight, d_offsets, d_gain, d_offset = lax.psum(
        (d_proj, d_table, d_weight, d_offsets, d_gain, d_offset), ("row", "col")
    )
    total_tokens = tokens.shape[0] * tokens.shape[1] * lax.axis_size("row") * lax.axis_size("col")
    out_scale = total_tokens ** (-0.5)
    d_tokens = (grad_out.astype(jnp.float32) + d_input).astype(jnp.bfloat16)
    return (
        d_tokens,
        d_weight * out_scale,
        d_offsets * out_scale,
        d_proj * out_scale,
        d_table * out_scale,
        d_gain * out_scale,
        d_offset * out_scale,
    )


def solution(mesh):
    placed = (
        P(("grp", "row"), "col", None),
        P(("grp", "row"), "col", None),
        P(("grp", "row"), "col"),
        P(),
        P(),
        P(),
        P(),
        P(),
        P(),
    )
    return jax.shard_map(
        on_device,
        mesh=mesh,
        in_specs=placed,
        out_specs=(
            P(("grp", "row"), "col", None),
            P("grp", None),
            P("grp"),
            P("grp", None),
            P("grp", None),
            P("grp"),
            P("grp"),
        ),
        check_vma=False,
    )
```

profile of v0, /device:TPU:0, one launch (start us, length us, event | category | flops | bytes accessed | tf_op | source)
XLA Modules:
  0.0 272.9 jit_solution(3321277854407880220)
XLA Ops:
  7.2 1.1 convert_reduce_fusion.1
  8.3 1.1 fusion.40
  9.5 0.6 copy-done.15
  10.1 1.6 multiply_convert_fusion
  12.1 6.0 %collective-permute-start = (bf16[4,128,540]{1,0,2:T(4,128)(2,1)S(1)}, bf16[4,128,540]{1,0,2:T(4,128)(2,1)S(1)}, u32[]{:S(2)}, u32[]{:S(2)}) collective-permute-start(bf16[4,128,540]{1,0,2:T(4,128)(2,1)S(1)} %copy.87), channel_id=1, source_target_pairs={{0,14},{2,0},{4,2},{6,4},{8,6},{10,8},{12,10},{14,12},{1,15},{3,1}... | collective-permute-start | bytes 1658888 | tf_op jit(solution)/shard_map/ppermute | solution.py:16
  18.2 0.6 collective-permute-start.2
  19.1 1.4 collective-permute-start.4
  20.7 0.6 copy-done.17
  21.3 2.6 fusion.2
  24.3 6.8 %collective-permute-done.2 = bf16[4,128]{1,0:T(4,128)(2,1)S(1)} collective-permute-done((bf16[4,128]{1,0:T(4,128)(2,1)S(1)}, bf16[4,128]{1,0:T(4,128)(2,1)S(1)}, u32[]{:S(2)}, u32[]{:S(2)}) %collective-permute-start.2) | collective-permute-done | bytes 1056 | tf_op jit(solution)/shard_map/ppermute | solution.py:16
  31.2 1.1 collective-permute-done.3
  32.9 2.7 %collective-permute-done.4 = bf16[4,128,180]{2,1,0:T(8,128)(2,1)S(1)} collective-permute-done((bf16[4,128,180]{2,1,0:T(8,128)(2,1)S(1)}, bf16[4,128,180]{2,1,0:T(8,128)(2,1)S(1)}, u32[]{:S(2)}, u32[]{:S(2)}) %collective-permute-start.4) | collective-permute-done | bytes 184352 | tf_op jit(solution)/shard_map/ppermute | solution.py:16
  35.8 1.0 collective-permute-done.5
  37.0 0.8 copy-done.2
  37.8 0.3 convolution_convert_fusion.3
  38.2 1.3 reshape.196
  39.7 0.5 copy.89
  40.4 0.4 slice_maximum_fusion
  40.7 0.7 collective-permute-done.1
  41.4 0.6 copy.90
  42.0 1.6 pad_maximum_fusion.3
  43.6 1.7 copy.91
  45.4 5.6 %reshape.191 = bf16[16,64,3,6,30]{4,3,2,1,0:T(8,128)(2,1)} reshape(bf16[16,8,8,540]{3,2,1,0:T(8,128)(2,1)S(1)} %copy.92) | data formatting | bytes 2211840 | tf_op jit(solution)/shard_map/while/body/eval_jaxpr/reshape;while/body/eval_jaxpr/reshape | solution.py:70
  51.1 6.6 %fusion.52 = (bf16[16,64,1,6,30]{4,3,2,1,0:T(8,128)(2,1)S(1)}, bf16[16,64,1,6,30]{4,3,2,1,0:T(8,128)(2,1)}, bf16[16,64,1,6,30]{4,3,2,1,0:T(8,128)(2,1)}) fusion(bf16[16,64,3,6,30]{4,3,2,1,0:T(8,128)(2,1)} %reshape.191), kind=kLoop, calls=%fused_computation.97 | loop fusion | bytes 2211840 | tf_op jit(solution)/shard_map/while/body/eval_jaxpr/slice | solution.py:73
  57.6 2.4 copy.123
  60.0 3.1 %copy.124 = bf16[16,64,1,6,30]{1,4,3,0,2:T(8,128)(2,1)} copy(bf16[16,64,1,6,30]{4,3,2,1,0:T(8,128)(2,1)} %get-tuple-element.77) | data formatting | bytes 737280
  63.2 1.9 copy.127
  65.1 1.7 fusion.26
  66.8 1.1 fusion.56
  68.2 1.0 multiply_reduce_fusion
  69.2 1.1 fusion.13
  70.3 0.5 fusion.12
  70.8 0.6 copy-done.1
  71.4 0.9 fusion.9
  72.4 0.9 fusion.10
  73.3 0.6 pad_maximum_fusion
  73.9 5.5 %copy.108 = bf16[16,64,3,6,30]{4,3,2,1,0:T(8,128)(2,1)} copy(bf16[16,64,3,6,30]{1,4,3,0,2:T(8,128)(2,1)S(1)} %pad_maximum_fusion) | data formatting | bytes 2211840 | tf_op jit(solution)/shard_map/while/body/eval_jaxpr/stack | solution.py:101
  79.4 7.9 %convert_element_type.55 = bf16[16,8,8,540]{3,2,1,0:T(8,128)(2,1)} reshape(bf16[16,64,3,6,30]{4,3,2,1,0:T(8,128)(2,1)} %copy.108) | data formatting | bytes 2211840 | tf_op jit(solution)/shard_map/while/body/eval_jaxpr/convert_element_type | solution.py:102
  87.3 1.4 copy_bitcast_fusion
  89.0 0.8 copy.128
  90.1 0.6 copy.112
  91.0 1.1 copy.113
  92.1 0.3 collective-permute-start.7
  92.4 0.4 copy-done.6
  92.8 1.5 fusion.11
  94.5 2.5 copy.116
  97.0 1.8 reshape.198
  98.8 1.4 fusion.1
  100.2 1.0 fusion.57
  101.2 9.2 %collective-permute-done.7 = bf16[4,128,540]{1,0,2:T(4,128)(2,1)} collective-permute-done((bf16[4,128,540]{1,0,2:T(4,128)(2,1)}, bf16[4,128,540]{1,0,2:T(4,128)(2,1)}, u32[]{:S(2)}, u32[]{:S(2)}) %collective-permute-start.7) | collective-permute-done | bytes 552992 | tf_op jit(solution)/shard_map/ppermute | solution.py:16
  110.4 1.1 copy.114
  111.6 0.6 convert_reduce_fusion
  112.2 0.4 copy-done.4
  112.6 0.7 fusion.39
  113.3 1.4 convolution_bitcast_fusion
  114.7 58.2 %all-reduce = (f32[540]{0:T(1024)S(1)}, f32[225,6]{0,1:T(8,128)S(1)}, f32[180]{0:T(256)S(1)}, f32[180]{0:T(256)S(1)}) all-reduce(f32[540]{0:T(1024)S(1)} %get-tuple-element.72, f32[225,6]{0,1:T(8,128)S(1)} %fusion.1, f32[180]{0:T(256)S(1)} %get-tuple-element.62, ...), channel_id=1, replica_groups=mesh['grp'=2,'row'=8,'col'=2] {'row','col'}, use_global_device_ids=true, to_apply=%region_9.10 | all-reduce | flops 2250 | bytes 18000 | tf_op jit(solution)/shard_map/psum | solution.py:206
  172.9 0.6 broadcast_multiply_fusion.3
  173.4 0.6 broadcast_multiply_fusion.7
  174.3 0.6 broadcast_multiply_fusion.8
  174.9 0.8 copy.118
  175.7 0.6 broadcast_multiply_fusion.2
  176.3 86.3 %all-reduce.4.cloned.1.call-done = (f32[180,540]{1,0:T(8,128)}, f32[180,180]{1,0:T(8,128)}) async-done(((f32[180,540]{1,0:T(8,128)}, f32[180,180]{1,0:T(8,128)}), (f32[180,540]{1,0:T(8,128)}, f32[180,180]{1,0:T(8,128)})) %all-reduce.4.cloned.1.call-update) | async-done | bytes 518416 | tf_op jit(solution)/shard_map/psum | solution.py:206
  262.6 1.8 broadcast_multiply_fusion
  264.5 1.6 broadcast_multiply_fusion.1
  (85 shorter events, 4.5 us)
Async XLA Ops:
  7.2 2.9 %copy-start = (bf16[180,540]{1,0:T(8,128)(2,1)S(1)}, bf16[180,540]{1,0:T(8,128)(2,1)}, u32[]{:S(2)}) copy-start(bf16[180,540]{1,0:T(8,128)(2,1)} %param.14) | copy-start | bytes 583204
  7.2 255.5 %all-reduce.4.cloned.1.call-start = ((), (), s32[]{:S(2)}) async-start(), calls=%async_computation | async-start | bytes 1318912 | tf_op jit(solution)/shard_map/psum | solution.py:206
  8.3 1.1 copy-start.13
  9.5 0.6 copy-start.15
  11.7 6.4 %copy-start.19 = (s32[8,128]{1,0:T(8,128)S(1)}, s32[8,128]{1,0:T(8,128)}, u32[]{:S(2)}) copy-start(s32[8,128]{1,0:T(8,128)} %param.11) | copy-start | bytes 12292
  11.7 7.0 %copy-start.7 = (bf16[8,128,180]{1,0,2:T(8,128)(2,1)S(1)}, bf16[8,128,180]{1,0,2:T(8,128)(2,1)}, u32[]{:S(2)}) copy-start(bf16[8,128,180]{1,0,2:T(8,128)(2,1)} %param.10) | copy-start | bytes 1105924
  11.7 9.5 %copy-start.21 = (f32[225,6]{0,1:T(8,128)S(1)}, f32[225,6]{0,1:T(8,128)}, u32[]{:S(2)}) copy-start(f32[225,6]{0,1:T(8,128)} %param.17) | copy-start | bytes 16204
  12.1 27.4 %collective-permute-start = (bf16[4,128,540]{1,0,2:T(4,128)(2,1)S(1)}, bf16[4,128,540]{1,0,2:T(4,128)(2,1)S(1)}, u32[]{:S(2)}, u32[]{:S(2)}) collective-permute-start(bf16[4,128,540]{1,0,2:T(4,128)(2,1)S(1)} %copy.87), channel_id=1, source_target_pairs={{0,14},{2,0},{4,2},{6,4},{8,6},{10,8},{12,10},{14,12},{1,15},{3,1}... | collective-permute-start | bytes 1658888 | tf_op jit(solution)/shard_map/ppermute | solution.py:16
  18.2 12.9 %collective-permute-start.2 = (bf16[4,128]{1,0:T(4,128)(2,1)S(1)}, bf16[4,128]{1,0:T(4,128)(2,1)S(1)}, u32[]{:S(2)}, u32[]{:S(2)}) collective-permute-start(bf16[4,128]{1,0:T(4,128)(2,1)S(1)} %get-tuple-element.84), channel_id=1, source_target_pairs={{0,14},{2,0},{4,2},{6,4},{8,6},{10,8},{12,10},{14,12},{1,15},{3,1}... | collective-permute-start | bytes 3080 | tf_op jit(solution)/shard_map/ppermute | solution.py:16
  19.1 16.5 %collective-permute-start.4 = (bf16[4,128,180]{2,1,0:T(8,128)(2,1)S(1)}, bf16[4,128,180]{2,1,0:T(8,128)(2,1)S(1)}, u32[]{:S(2)}, u32[]{:S(2)}) collective-permute-start(bf16[4,128,180]{2,1,0:T(8,128)(2,1)S(1)} %copy.126), channel_id=1, source_target_pairs={{0,14},{2,0},{4,2},{6,4},{8,6},{10,8},{12,10},{14,12},{1,15},{3,1}... | collective-permute-start | bytes 552968 | tf_op jit(solution)/shard_map/ppermute | solution.py:16
  20.7 0.6 copy-start.17
  24.1 13.8 %copy-start.12 = (bf16[180,180]{1,0:T(8,128)(2,1)S(1)}, bf16[180,180]{1,0:T(8,128)(2,1)}, u32[]{:S(2)}) copy-start(bf16[180,180]{1,0:T(8,128)(2,1)} %param.16) | copy-start | bytes 194404
  31.1 1.2 collective-permute-start.3
  35.6 1.2 collective-permute-start.5
  37.0 0.8 copy-start.2
  40.1 1.3 collective-permute-start.1
  66.8 1.1 copy-start.9
  66.8 1.3 copy-start.11
  67.9 4.4 %copy-start.5 = (f32[16,6,64,64]{2,3,1,0:T(8,128)}, f32[16,6,64,64]{2,3,1,0:T(8,128)S(1)}, u32[]{:S(2)}) copy-start(f32[16,6,64,64]{2,3,1,0:T(8,128)S(1)} %get-tuple-element.86) | copy-start | bytes 4718596
  70.3 1.1 copy-start.1
  88.8 1.3 collective-permute-start.6
  90.1 2.3 copy-start.10
  90.6 2.2 copy-start.6
  92.1 18.4 %collective-permute-start.7 = (bf16[4,128,540]{1,0,2:T(4,128)(2,1)}, bf16[4,128,540]{1,0,2:T(4,128)(2,1)}, u32[]{:S(2)}, u32[]{:S(2)}) collective-permute-start(bf16[4,128,540]{1,0,2:T(4,128)(2,1)} %copy.113), channel_id=1, source_target_pairs={{0,2},{2,4},{4,6},{6,8},{8,10},{10,12},{12,14},{14,0},{1,3},{3,5},... | collective-permute-start | bytes 1658888 | tf_op jit(solution)/shard_map/ppermute | solution.py:16
  94.3 4.5 %copy-start.18 = (s32[4096]{0:T(1024)S(1)}, s32[4096]{0:T(1024)}, u32[]{:S(2)}) copy-start(s32[4096]{0:T(1024)} %copy-done.17) | copy-start | bytes 49156
  94.4 5.8 %copy-start.3 = (bf16[16,8,8,180]{3,2,1,0:T(8,128)(2,1)S(1)}, bf16[16,8,8,180]{3,2,1,0:T(8,128)(2,1)}, u32[]{:S(2)}) copy-start(bf16[16,8,8,180]{3,2,1,0:T(8,128)(2,1)} %copy-done.2) | copy-start | bytes 1105924
  111.6 1.0 copy-start.4
  111.6 1.0 copy-start.14
  111.6 1.0 copy-start.16
  111.6 1.0 copy-start.20
  112.2 1.1 copy-start.22
  113.3 60.8 %copy-start.8 = (bf16[8,128,180]{1,0,2:T(8,128)(2,1)S(1)}, bf16[8,128,180]{1,0,2:T(8,128)(2,1)}, u32[]{:S(2)}) copy-start(bf16[8,128,180]{1,0,2:T(8,128)(2,1)} %param.10) | copy-start | bytes 1105924
Sparse Core Ops, SparseCore 0:
  174.2 88.4 all-reduce.3
where the time goes:
time: 274 us; the launch traced here: 273 us
  waiting for transfers between devices  108 us (39%)
  blocking collectives  58.2 us (21%)
  local copies, waits for them, and re-layouts  52.8 us (19%)
  matrix products  15.6 us (6%)
  other arithmetic  14.7 us (5%)
  between operations  14.5 us (5%)
  starting transfers between devices  8.96 us (3%)
    psum x1, waiting for transfers between devices, on_device(): lax.psum((d_proj, d_table, d_weight, d_offsets, d_gain, d_offset), ('row'...  86.3 us
    psum x1, blocking collectives, on_device(): lax.psum((d_proj, d_table, d_weight, d_offsets, d_gain, d_offset), ('row'...  58.2 us
    ppermute x8, waiting for transfers between devices, from_behind(): lax.ppermute(shard, axis, [(i, (i + by) % count) for i in range(count)])  21.8 us
    unnamed x53, local copies, waits for them, and re-layouts  13.1 us
    dot_general x11, matrix products, multiply(): return jnp.einsum(form, left, right, preferred_element_type=jnp.float32)  11.6 us
    ppermute x8, starting transfers between devices, from_behind(): lax.ppermute(shard, axis, [(i, (i + by) % count) for i in range(count)])  8.92 us
    convert_element_type x1, local copies, waits for them, and re-layouts, window_band(): d_qkv = jnp.stack([d_query, d_key, d_value], 2).astype(jnp.bfloat16).resh...  7.91 us
    slice x1, local copies, waits for them, and re-layouts, window_band(): value_part = parted[:, :, 2]  6.55 us
  transfers between devices with their start and end apart: 9, of which 8 were waited for; matrix products, arithmetic and copies ran while one was open for 7% of the time, Pallas kernels for 0%

commit v1 on v0

v1 whole, which is shorter than its diff:
```python
import functools

import jax
import jax.numpy as jnp
from jax import lax
from jax.experimental import pallas as pl
from jax.experimental.pallas import tpu as pltpu
from jax.sharding import PartitionSpec as P

HEADS = 6
WIN = 8
SHIFT = 4
SPAN = WIN * WIN
C = 180
HEAD = C // HEADS
LANES = HEADS * SPAN
BLOCK = 184
EDGE = 16
MASKED = -10000.0
MESH = pl.DeviceIdType.MESH
F32 = jnp.float32
BF16 = jnp.bfloat16

NN = (((1,), (0,)), ((), ()))
NT = (((1,), (1,)), ((), ()))
TN = (((0,), (0,)), ((), ()))


def mul(left, right, form=NN):
    return lax.dot_general(left, right, form, preferred_element_type=F32)


def exact(left, right, form=NN):
    return lax.dot_general(
        left, right, form, preferred_element_type=F32, precision=lax.Precision.HIGHEST
    )


def iota(shape, dim):
    return lax.broadcasted_iota(jnp.int32, shape, dim)


def col_spread(cj):
    src = iota((SPAN, 128), 0)
    dst = iota((SPAN, 128), 1)
    return (dst == (src >> 3) * 16 + (src & 7) - cj + 7).astype(F32)


def row_spread(rj):
    src = iota((128, 256), 0)
    dst = iota((128, 256), 1)
    return (dst == src + 16 * (7 - rj)).astype(F32)


def table_spread(entries):
    src = iota((entries, 256), 0)
    dst = iota((entries, 256), 1)
    hit = (src == (dst >> 4) * 15 + (dst & 15)) & ((dst & 15) < 15) & (dst < 240)
    return hit.astype(F32)


def body(
    rows_n, cols_n, rows_total, out_scale,
    tok, grad, reg, gain_ref, offset_ref, qkvw, qkvb, projw, table,
    d_tok, d_qkvw, d_qkvb, d_projw, d_table, d_ln,
    tok_b, tok_r, tok_d, grad_b, grad_r, grad_d, reg_b, reg_r,
    unit, inv_std, gradf, normed, q_s, k_s, v_s, da_s, gb_s, att, dq_s, dk_s, dv_s,
    bias_t, span_a, span_b, hmask, lab_col, lab_row, score_acc,
    frame, frame_low, back_u, back_l, back_ul,
    pack, pack_low, pair_in, half_low, part_in, result,
    halo_send, halo_recv, back_send, back_recv, pair_sem,
    part_send, part_recv, all_send, all_recv, fwd_send, fwd_recv,
):
    row = lax.axis_index("row")
    col = lax.axis_index("col")
    up = lax.rem(row + rows_n - 1, rows_n)
    down = lax.rem(row + 1, rows_n)
    other = lax.rem(col + 1, cols_n)
    tile_cols = tok.shape[1]
    wins = tile_cols // WIN
    count = wins * SPAN
    half = rows_total // 2
    chunk = half // rows_n

    def remote(src, dst, send, recv, to_row, to_col):
        return pltpu.make_async_remote_copy(
            src_ref=src, dst_ref=dst, send_sem=send, recv_sem=recv,
            device_id={"row": to_row, "col": to_col}, device_id_type=MESH,
        )

    barrier = pltpu.get_barrier_semaphore()

    @pl.loop(1, rows_n)
    def _(k):
        pl.semaphore_signal(
            barrier, inc=1, device_id={"row": lax.rem(row + k, rows_n), "col": col},
            device_id_type=MESH,
        )

    for to_row in (row, up, down):
        pl.semaphore_signal(
            barrier, inc=1, device_id={"row": to_row, "col": other}, device_id_type=MESH
        )
    pl.semaphore_wait(barrier, rows_n + 2)

    halos = []
    for src, dst, to_row, to_col in (
        (reg, reg_b, up, col),
        (reg, reg_r, row, other),
        (tok.at[0:SHIFT], tok_b, up, col),
        (tok.at[SHIFT:WIN, 0:EDGE], tok_r, row, other),
        (tok.at[0:SHIFT, 0:EDGE], tok_d, up, other),
        (grad.at[0:SHIFT], grad_b, up, col),
        (grad.at[SHIFT:WIN, 0:EDGE], grad_r, row, other),
        (grad.at[0:SHIFT, 0:EDGE], grad_d, up, other),
    ):
        i = len(halos)
        halos.append(remote(src, dst, halo_send.at[i], halo_recv.at[i], to_row, to_col))
        halos[-1].start()

    flat = exact(table[...], table_spread(table.shape[0]), TN)
    for rj in range(WIN):
        span_b[pl.ds(rj, HEADS, stride=WIN), :] = exact(flat, row_spread(rj), NT)
    for cj in range(WIN):
        span_a[pl.ds(cj, HEADS * WIN, stride=WIN), :] = exact(span_b[...], col_spread(cj), NT)
    for h in range(HEADS):
        bias_t[:, h * SPAN : (h + 1) * SPAN] = span_a[h * SPAN : (h + 1) * SPAN, :]
    mask_row = iota((LANES, C), 0) >> 6
    mask_col = iota((LANES, C), 1)
    hmask[...] = (
        (mask_col >= mask_row * HEAD) & (mask_col < (mask_row + 1) * HEAD)
    ).astype(F32).astype(BF16)
    score_acc[...] = jnp.zeros_like(score_acc)
    pack[...] = jnp.zeros_like(pack)

    for copy in halos:
        copy.wait()

    own = reg[...]
    row_part = jnp.concatenate([own[SHIFT:], reg_b[0:SHIFT, :]], 0)[:, 0:1] >> 2
    col_own = pltpu.roll(own, tile_cols - SHIFT, 1)
    col_right = pltpu.roll(reg_r[...], tile_cols - SHIFT, 1)
    col_part = jnp.where(iota((WIN, tile_cols), 1) < tile_cols - SHIFT, col_own, col_right)[0:1] & 3
    label = (row_part * 4 + col_part).astype(F32)
    spread = jnp.broadcast_to(label[:, None, :], (WIN, WIN, tile_cols)).reshape(SPAN, tile_cols)
    spread = jnp.where(
        (iota((SPAN, tile_cols), 0) & 7) == (iota((SPAN, tile_cols), 1) & 7), spread, 0.0
    )
    pick = ((iota((tile_cols, wins), 0) >> 3) == iota((tile_cols, wins), 1)).astype(F32)
    columns = exact(spread, pick)
    tiled = (iota((SPAN, LANES), 0) == (iota((SPAN, LANES), 1) & (SPAN - 1))).astype(F32)
    lab_row[...] = exact(columns, tiled, TN)
    for w in range(wins):
        lab_col[w] = jnp.broadcast_to(columns[:, w : w + 1], (SPAN, 128))

    for main, below, right, diag, target in (
        (tok, tok_b, tok_r, tok_d, unit),
        (grad, grad_b, grad_r, grad_d, gradf),
    ):
        for r in range(WIN):
            if r < SHIFT:
                left_part, right_part = main[r + SHIFT], right[r]
            else:
                left_part, right_part = below[r - SHIFT], diag[r - SHIFT]
            wide = jnp.concatenate([left_part.astype(F32), right_part.astype(F32)], 0)
            target[:, r] = wide[SHIFT : SHIFT + tile_cols].reshape(wins, WIN, C)

    step_wins = 4
    step = step_wins * SPAN
    steps = wins // step_wins

    @pl.loop(0, steps)
    def _(s):
        at = pl.ds(pl.multiple_of(s * step, step), step)
        win_at = pl.ds(s * step_wins, step_wins)
        x = unit[win_at].reshape(step, C)
        center = jnp.mean(x, -1, keepdims=True)
        x = x - center
        inv = lax.rsqrt(jnp.mean(x * x, -1, keepdims=True) + 1e-05)
        x = x * inv
        unit[win_at] = x.reshape(step_wins, WIN, WIN, C)
        inv_std[at] = inv
        n = (x * gain_ref[...] + offset_ref[...]).astype(BF16)
        normed[at] = n
        q_s[at] = ((mul(n, qkvw[0]) + qkvb[0]) * HEAD ** (-0.5)).astype(BF16)
        k_s[at] = (mul(n, qkvw[1]) + qkvb[1]).astype(BF16)
        v_s[at] = (mul(n, qkvw[2]) + qkvb[2]).astype(BF16)
        g = gradf[win_at].reshape(step, C).astype(BF16)
        gb_s[at] = g
        da_s[at] = mul(g, projw[...], NT).astype(BF16)

    def gather_heads(stacked):
        kept = stacked * hmask[...].astype(F32)
        return jnp.sum(kept.reshape(HEADS, SPAN, C), 0)

    @pl.loop(0, wins)
    def _(w):
        at = pl.ds(pl.multiple_of(w * SPAN, SPAN), SPAN)
        q, k, v, da = q_s[at], k_s[at], v_s[at], da_s[at]
        heads = hmask[...]
        qm = jnp.concatenate([q] * HEADS, 0) * heads
        dam = jnp.concatenate([da] * HEADS, 0) * heads
        same = lab_col[w][:, 0:1] == lab_row[pl.ds(w, 1), :]
        scores = jnp.where(same, mul(k, qm, NT) + bias_t[...], MASKED)
        e = jnp.exp(scores - jnp.max(scores, 0, keepdims=True))
        p = e * (1.0 / jnp.sum(e, 0, keepdims=True))
        p_low = p.astype(BF16)
        att[at] = gather_heads(mul(p_low, v, TN)).astype(BF16)
        dp = mul(v, dam, NT)
        ds = p * (dp - jnp.sum(p * dp, 0, keepdims=True))
        score_acc[...] += ds
        ds_low = ds.astype(BF16)
        dq_s[at] = (gather_heads(mul(ds_low, k, TN)) * HEAD ** (-0.5)).astype(BF16)
        dk_s[at] = mul(ds_low, qm).astype(BF16)
        dv_s[at] = mul(p_low, dam).astype(BF16)

    small = 4 * BLOCK

    @pl.loop(0, steps)
    def _(s):
        at = pl.ds(pl.multiple_of(s * step, step), step)
        win_at = pl.ds(s * step_wins, step_wins)
        x = unit[win_at].reshape(step, C)
        dn = mul(dq_s[at], qkvw[0], NT) + mul(dk_s[at], qkvw[1], NT) + mul(dv_s[at], qkvw[2], NT)
        pack[small + 3 : small + 4, 0:C] += jnp.sum(dn * x, 0, keepdims=True)
        pack[small + 4 : small + 5, 0:C] += jnp.sum(dn, 0, keepdims=True)
        g = dn * gain_ref[...]
        dx = inv_std[at] * (
            g - jnp.mean(g, -1, keepdims=True) - x * jnp.mean(g * x, -1, keepdims=True)
        )
        out = gradf[win_at].reshape(step, C) + dx
        out = out.reshape(step_wins, WIN, WIN, C)
        for i in range(step_wins):
            frame[:, pl.ds(s * step_wins + i, 1)] = out[i][:, None]

    for r in range(WIN):
        frame_low[r] = frame[r].reshape(tile_cols, C).astype(BF16)

    edge = tile_cols - EDGE
    backs = []
    for src, dst, to_row, to_col in (
        (frame_low.at[SHIFT:WIN], back_u, down, col),
        (frame_low.at[0:SHIFT, edge:tile_cols], back_l, row, other),
        (frame_low.at[SHIFT:WIN, edge:tile_cols], back_ul, down, other),
    ):
        i = len(backs)
        backs.append(remote(src, dst, back_send.at[i], back_recv.at[i], to_row, to_col))
        backs[-1].start()

    ones = jnp.ones((8, count), BF16)
    for i, part in enumerate((dq_s, dk_s, dv_s)):
        pack[i * BLOCK : i * BLOCK + C, 0:C] = mul(normed[...], part[...], TN)
        pack[small + i : small + i + 1, 0:C] = mul(ones, part[...])[0:1]
    pack[3 * BLOCK : 3 * BLOCK + C, 0:C] = mul(att[...], gb_s[...], TN)
    for h in range(HEADS):
        span_a[h * SPAN : (h + 1) * SPAN, :] = score_acc[:, h * SPAN : (h + 1) * SPAN]
    folded = jnp.zeros((HEADS * WIN, 128), F32)
    for cj in range(WIN):
        folded += exact(span_a[pl.ds(cj, HEADS * WIN, stride=WIN), :], col_spread(cj))
    span_b[...] = folded
    flat_sum = jnp.zeros((HEADS, 256), F32)
    for rj in range(WIN):
        flat_sum += exact(span_b[pl.ds(rj, HEADS, stride=WIN), :], row_spread(rj))
    pack[small + 8 : small + 8 + HEADS, :] = flat_sum
    pack_low[...] = pack[...].astype(BF16)

    pair = remote(
        pack_low.at[pl.ds(pl.multiple_of(other * half, 16), half)], pair_in,
        pair_sem.at[0], pair_sem.at[1], row, other,
    )
    pair.start()
    pair.wait()
    mine = pl.ds(pl.multiple_of(col * half, 16), half)
    half_low[...] = (pack[mine] + pair_in[...].astype(F32)).astype(BF16)

    def part_copy(k):
        peer = lax.rem(row + k, rows_n)
        return remote(
            half_low.at[pl.ds(pl.multiple_of(peer * chunk, 16), chunk)], part_in.at[k],
            part_send.at[k], part_recv.at[k], peer, col,
        )

    @pl.loop(1, rows_n)
    def _(k):
        part_copy(k).start()

    def add_part(k, total):
        part_copy(k).wait()
        return total + part_in[k].astype(F32)

    my_chunk = pl.ds(pl.multiple_of(row * chunk, 16), chunk)
    total = lax.fori_loop(1, rows_n, add_part, half_low[my_chunk].astype(F32))
    own_chunk = result.at[col, my_chunk]
    own_chunk[...] = total.astype(BF16)

    def all_copy(k):
        return remote(
            own_chunk, own_chunk, all_send.at[k], all_recv.at[k],
            lax.rem(row + k, rows_n), col,
        )

    def forward(k):
        source = lax.rem(row + rows_n - k, rows_n)
        piece = result.at[col, pl.ds(pl.multiple_of(source * chunk, 16), chunk)]
        return remote(piece, piece, fwd_send.at[k], fwd_recv.at[k], row, other)

    @pl.loop(1, rows_n)
    def _(k):
        all_copy(k).start()

    forward(0).start()

    for copy in backs:
        copy.wait()
    for r in range(WIN):
        if r < SHIFT:
            left_part, main_part = back_ul[r], back_u[r]
        else:
            left_part, main_part = back_l[r - SHIFT], frame_low[r - SHIFT]
        wide = jnp.concatenate([left_part.astype(F32), main_part.astype(F32)], 0)
        d_tok[r] = wide[EDGE - SHIFT : EDGE - SHIFT + tile_cols].astype(BF16)

    @pl.loop(1, rows_n)
    def _(k):
        all_copy(k).wait()
        forward(k).start()

    @pl.loop(0, rows_n)
    def _(k):
        forward(k).wait()

    pack[0:half] = result[0].astype(F32) * out_scale
    pack[half : 2 * half] = result[1].astype(F32) * out_scale
    for i in range(3):
        d_qkvw[i] = pack[i * BLOCK : i * BLOCK + C, 0:C]
        d_qkvb[i] = pack[small + i : small + i + 1, 0:C]
    d_projw[...] = pack[3 * BLOCK : 3 * BLOCK + C, 0:C]
    d_ln[...] = pack[small + 3 : small + 5, 0:C]
    entries = table_spread(d_table.shape[0])
    d_table[...] = exact(entries, pack[small + 8 : small + 8 + HEADS, :], NT)


def on_device(
    tokens, grad_out, regions, ln_gain, ln_offset, qkv_weight, qkv_bias, proj_weight, bias_table
):
    rows_n, cols_n = lax.axis_size("row"), lax.axis_size("col")
    tile_cols = tokens.shape[1]
    wins = tile_cols // WIN
    count = wins * SPAN
    unit_rows = 2 * 16 * rows_n
    needed = 4 * BLOCK + 16
    rows_total = -(-needed // unit_rows) * unit_rows
    half = rows_total // 2
    chunk = half // rows_n
    total_tokens = tokens.shape[0] * tile_cols * rows_n * cols_n
    split_w = qkv_weight.reshape(C, 3, C).transpose(1, 0, 2)
    vmem = pltpu.VMEM
    halo = [
        vmem((SHIFT, tile_cols, C), BF16),
        vmem((SHIFT, EDGE, C), BF16),
        vmem((SHIFT, EDGE, C), BF16),
    ]
    flat_low = vmem((count, C), BF16)
    whole = pl.BlockSpec(memory_space=pltpu.VMEM)
    dma = pltpu.SemaphoreType.DMA
    outs = pl.pallas_call(
        functools.partial(body, rows_n, cols_n, rows_total, total_tokens ** (-0.5)),
        out_shape=(
            jax.ShapeDtypeStruct(tokens.shape, BF16),
            jax.ShapeDtypeStruct((3, C, C), F32),
            jax.ShapeDtypeStruct((3, 1, C), F32),
            jax.ShapeDtypeStruct((C, C), F32),
            jax.ShapeDtypeStruct(bias_table.shape, F32),
            jax.ShapeDtypeStruct((2, C), F32),
        ),
        in_specs=[whole] * 9,
        out_specs=(whole,) * 6,
        scratch_shapes=halo + halo + [
            vmem(regions.shape, jnp.int32),
            vmem(regions.shape, jnp.int32),
            vmem((wins, WIN, WIN, C), F32),
            vmem((count, 1), F32),
            vmem((wins, WIN, WIN, C), F32),
        ] + [flat_low] * 10 + [
            vmem((SPAN, LANES), F32),
            vmem((HEADS * SPAN, SPAN), F32),
            vmem((HEADS * WIN, 128), F32),
            vmem((LANES, C), BF16),
            vmem((wins, SPAN, 128), F32),
            vmem((wins, LANES), F32),
            vmem((SPAN, LANES), F32),
            vmem((WIN, wins, WIN, C), F32),
            vmem((WIN, tile_cols, C), BF16),
        ] + halo + [
            vmem((rows_total, 256), F32),
            vmem((rows_total, 256), BF16),
            vmem((half, 256), BF16),
            vmem((half, 256), BF16),
            vmem((rows_n, chunk, 256), BF16),
            vmem((2, half, 256), BF16),
            dma((8,)), dma((8,)), dma((3,)), dma((3,)), dma((2,)),
            dma((rows_n,)), dma((rows_n,)), dma((rows_n,)), dma((rows_n,)),
            dma((rows_n,)), dma((rows_n,)),
        ],
        compiler_params=pltpu.CompilerParams(
            collective_id=0, has_side_effects=True, vmem_limit_bytes=48 * 1024 * 1024
        ),
    )(
        tokens, grad_out, regions, ln_gain.reshape(1, C), ln_offset.reshape(1, C), split_w,
        qkv_bias.reshape(3, 1, C), proj_weight, bias_table,
    )
    d_tokens, d_qkvw, d_qkvb, d_projw, d_table, d_ln = outs
    return (
        d_tokens,
        d_qkvw.transpose(1, 0, 2).reshape(C, 3 * C),
        d_qkvb.reshape(3 * C),
        d_projw,
        d_table,
        d_ln[0],
        d_ln[1],
    )


def solution(mesh):
    placed = (
        P(("grp", "row"), "col", None),
        P(("grp", "row"), "col", None),
        P(("grp", "row"), "col"),
        P(),
        P(),
        P(),
        P(),
        P(),
        P(),
    )
    return jax.shard_map(
        on_device,
        mesh=mesh,
        in_specs=placed,
        out_specs=(
            P(("grp", "row"), "col", None),
            P("grp", None),
            P("grp"),
            P("grp", None),
            P("grp", None),
            P("grp"),
            P("grp"),
        ),
        check_vma=False,
    )
```

time: 274 us -> 70.7 us (0.26)
  waiting for transfers between devices: 108 us -> 0 us
  Pallas kernels: 0 us -> 59.7 us
  blocking collectives: 58.2 us -> 0 us
  local copies, waits for them, and re-layouts: 52.8 us -> 9.96 us
  matrix products: 15.6 us -> 0 us
  other arithmetic: 14.7 us -> 0.02 us
  between operations: 14.5 us -> 0.71 us
  starting transfers between devices: 8.96 us -> 0 us
    psum x1 -> x0, waiting for transfers between devices: 86.3 us -> none  [on_device(): lax.psum((d_proj, d_table, d_weight, d_offsets, d_gain, d_offset), ('row'...]
    pallas_call x0 -> x1, Pallas kernels: none -> 59.7 us  [on_device(): pl.pallas_call(functools.partial(body, rows_n, cols_n, rows_total, total_...]
    psum x1 -> x0, blocking collectives: 58.2 us -> none  [on_device(): lax.psum((d_proj, d_table, d_weight, d_offsets, d_gain, d_offset), ('row'...]
    ppermute x8 -> x0, waiting for transfers between devices: 21.8 us -> none  [from_behind(): lax.ppermute(shard, axis, [(i, (i + by) % count) for i in range(count)])]
    dot_general x13 -> x0, matrix products: 15.6 us -> none  [the longest x11 11.6 us: multiply(): return jnp.einsum(form, left, right, preferred_element_type=jnp.float32)]
    convert_element_type x2 -> x0, local copies, waits for them, and re-layouts: 10.4 us -> none  [the longest x1 7.91 us: window_band(): d_qkv = jnp.stack([d_query, d_key, d_value], 2).astype(jnp.bfloat16).resh...]
    ppermute x8 -> x0, starting transfers between devices: 8.92 us -> none  [from_behind(): lax.ppermute(shard, axis, [(i, (i + by) % count) for i in range(count)])]
    slice x10 -> x1, local copies, waits for them, and re-layouts: 8.73 us -> 0.57 us  [on_device(): d_ln[1]]
  transfers between devices with their start and end apart: 9 -> 0, of which waited for: 8 -> 0; matrix products, arithmetic and copies ran while one was open for 7% -> 0% of each run, Pallas kernels for 0% -> 0%
where the time goes in v1:
time: 70.7 us; the launch traced here: 70.4 us
  Pallas kernels  59.7 us (84%)
  local copies, waits for them, and re-layouts  9.96 us (14%)
  between operations  0.71 us (1%)
    pallas_call x1, Pallas kernels, on_device(): pl.pallas_call(functools.partial(body, rows_n, cols_n, rows_total, total_...  59.7 us
    unnamed x22, local copies, waits for them, and re-layouts  6.72 us

profile of v1, /device:TPU:0, one launch (start us, length us, event | category | flops | bytes accessed | tf_op | source)
XLA Modules:
  0.0 70.4 jit_solution(5793750409520260817)
XLA Ops:
  0.6 0.0 copy-start.6
  0.6 0.8 %reshape.35.qkvb = f32[3,1,180]{2,1,0:T(1,128)S(1)} reshape(f32[540]{0:T(1024)} %param.15) | data formatting | bytes 4320 | tf_op jit(solution)/shard_map/reshape | solution.py:410
  1.4 0.0 copy-done.6
  1.4 0.1 copy.25.table
  1.6 1.2 %reshape.38 = bf16[180,3,180]{2,1,0:T(4,128)(2,1)S(1)} reshape(bf16[180,540]{1,0:T(8,128)(2,1)} %param.14) | data formatting | bytes 388800 | tf_op jit(solution)/shard_map/reshape | solution.py:356
  2.8 0.0 copy-start.4
  2.8 0.9 %copy-done.4 = bf16[8,128,180]{1,0,2:T(8,128)(2,1)S(1)} copy-done((bf16[8,128,180]{1,0,2:T(8,128)(2,1)S(1)}, bf16[8,128,180]{1,0,2:T(8,128)(2,1)}, u32[]{:S(2)}) %copy-start.4) | copy-done | bytes 368664
  3.7 0.0 copy-start.5
  3.8 0.3 copy.23.tok
  4.1 0.7 copy-done.5
  4.7 0.0 copy-start
  4.7 0.0 copy-start.1
  4.7 0.0 copy-start.2
  4.7 0.0 copy-start.3
  4.7 0.3 copy.24.grad
  5.0 0.6 copy-done
  5.6 0.0 copy-done.1
  5.6 0.0 copy-done.2
  5.6 0.0 copy-done.3
  5.6 59.7 %shard_map.144 = (bf16[8,128,180]{2,1,0:T(8,128)(2,1)S(1)}, f32[3,180,180]{2,1,0:T(8,128)S(1)}, f32[3,1,180]{2,1,0:T(1,128)S(1)}, f32[180,180]{1,0:T(8,128)S(1)}...) custom-call(bf16[8,128,180]{2,1,0:T(8,128)(2,1)S(1)} %copy.23.tok, bf16[8,128,180]{2,1,0:T(8,128)(2,1)S(1)} %copy.24.grad, ...), custom_call_target="tpu_custom_call" | custom-call | tf_op jit(solution)/shard_map/pallas_call | solution.py:366
  65.4 1.0 %copy.27 = bf16[8,128,180]{1,0,2:T(8,128)(2,1)} copy(bf16[8,128,180]{2,1,0:T(8,128)(2,1)S(1)} %get-tuple-element.26) | data formatting | bytes 737280
  66.4 0.6 fusion
  66.9 0.7 reshape.37
  67.6 0.7 copy.29
  68.3 0.3 copy.32
  68.6 1.1 %reshape.39 = f32[180,540]{1,0:T(8,128)} reshape(f32[180,3,180]{2,1,0:T(4,128)S(1)} %copy.32) | data formatting | bytes 777600
  69.7 0.7 copy.37
  (2 shorter events, 0.1 us)
Async XLA Ops:
  0.6 0.8 %copy-start.6 = (f32[225,6]{0,1:T(8,128)S(1)}, f32[225,6]{0,1:T(8,128)}, u32[]{:S(2)}) copy-start(f32[225,6]{0,1:T(8,128)} %param.17) | copy-start | bytes 16204
  2.8 1.0 %copy-start.4 = (bf16[8,128,180]{1,0,2:T(8,128)(2,1)S(1)}, bf16[8,128,180]{1,0,2:T(8,128)(2,1)}, u32[]{:S(2)}) copy-start(bf16[8,128,180]{1,0,2:T(8,128)(2,1)} %param.9) | copy-start | bytes 1105924
  3.7 1.0 %copy-start.5 = (bf16[8,128,180]{1,0,2:T(8,128)(2,1)S(1)}, bf16[8,128,180]{1,0,2:T(8,128)(2,1)}, u32[]{:S(2)}) copy-start(bf16[8,128,180]{1,0,2:T(8,128)(2,1)} %param.10) | copy-start | bytes 1105924
  4.7 0.9 %copy-start = (bf16[180,180]{1,0:T(8,128)(2,1)S(1)}, bf16[180,180]{1,0:T(8,128)(2,1)}, u32[]{:S(2)}) copy-start(bf16[180,180]{1,0:T(8,128)(2,1)} %projw.1) | copy-start | bytes 194404
  4.7 0.9 %copy-start.1 = (s32[8,128]{1,0:T(8,128)S(1)}, s32[8,128]{1,0:T(8,128)}, u32[]{:S(2)}) copy-start(s32[8,128]{1,0:T(8,128)} %reg.1) | copy-start | bytes 12292
  4.7 0.9 %copy-start.2 = (f32[180]{0:T(256)S(1)}, f32[180]{0:T(256)}, u32[]{:S(2)}) copy-start(f32[180]{0:T(256)} %param.12) | copy-start | bytes 2164
  4.7 0.9 %copy-start.3 = (f32[180]{0:T(256)S(1)}, f32[180]{0:T(256)}, u32[]{:S(2)}) copy-start(f32[180]{0:T(256)} %param.13) | copy-start | bytes 2164

commit v2 on v1

v2 whole, which is shorter than its diff:
```python
import functools

import jax
import jax.numpy as jnp
from jax import lax
from jax.experimental import pallas as pl
from jax.experimental.pallas import tpu as pltpu
from jax.sharding import PartitionSpec as P

HEADS = 6
WIN = 8
SHIFT = 4
SPAN = WIN * WIN
C = 180
HEAD = C // HEADS
LANES = HEADS * SPAN
BLOCK = 184
EDGE = 16
MASKED = -10000.0
MESH = pl.DeviceIdType.MESH
F32 = jnp.float32
BF16 = jnp.bfloat16

NN = (((1,), (0,)), ((), ()))
NT = (((1,), (1,)), ((), ()))
TN = (((0,), (0,)), ((), ()))


def mul(left, right, form=NN):
    return lax.dot_general(left, right, form, preferred_element_type=F32)


def exact(left, right, form=NN):
    return lax.dot_general(
        left, right, form, preferred_element_type=F32, precision=lax.Precision.HIGHEST
    )


def split_mul(left, picks):
    high = left.astype(BF16)
    low = (left - high.astype(F32)).astype(BF16)
    return mul(high, picks) + mul(low, picks)


def iota(shape, dim):
    return lax.broadcasted_iota(jnp.int32, shape, dim)


def col_spread(cj):
    src = iota((SPAN, 128), 0)
    dst = iota((SPAN, 128), 1)
    return (dst == (src >> 3) * 16 + (src & 7) - cj + 7).astype(F32)


def row_spread(rj):
    src = iota((128, 256), 0)
    dst = iota((128, 256), 1)
    return (dst == src + 16 * (7 - rj)).astype(F32)


def table_spread(entries):
    src = iota((entries, 256), 0)
    dst = iota((entries, 256), 1)
    hit = (src == (dst >> 4) * 15 + (dst & 15)) & ((dst & 15) < 15) & (dst < 240)
    return hit.astype(F32)


def body(
    rows_n, cols_n, rows_total, out_scale,
    tok, grad, reg, gain_ref, offset_ref, qkvw, qkvb, projw, table,
    d_tok, d_qkvw, d_qkvb, d_projw, d_table, d_gain, d_offset,
    tok_b, tok_r, tok_d, grad_b, grad_r, grad_d, reg_b, reg_r,
    unit, inv_std, gradf, nt_s, q_s, k_s, v_s, da_s, gb_s, att, dq_s, dk_s, dv_s,
    w_s, b_s, bias_t, span_a, span_b, hmask, lab_col, lab_row, score_acc,
    fold_a, fold_b, frame_low, back_u, back_l, back_ul,
    pack, pack_low, pair_in, half_low, part_in, result,
    halo_send, halo_recv, back_send, back_recv, pair_sem,
    part_send, part_recv, all_send, all_recv, fwd_send, fwd_recv,
):
    row = lax.axis_index("row")
    col = lax.axis_index("col")
    up = lax.rem(row + rows_n - 1, rows_n)
    down = lax.rem(row + 1, rows_n)
    other = lax.rem(col + 1, cols_n)
    tile_cols = tok.shape[1]
    wins = tile_cols // WIN
    count = wins * SPAN
    half = rows_total // 2
    chunk = half // rows_n

    def remote(src, dst, send, recv, to_row, to_col):
        return pltpu.make_async_remote_copy(
            src_ref=src, dst_ref=dst, send_sem=send, recv_sem=recv,
            device_id={"row": to_row, "col": to_col}, device_id_type=MESH,
        )

    barrier = pltpu.get_barrier_semaphore()

    @pl.loop(1, rows_n)
    def _(k):
        pl.semaphore_signal(
            barrier, inc=1, device_id={"row": lax.rem(row + k, rows_n), "col": col},
            device_id_type=MESH,
        )

    for to_row in (row, up, down):
        pl.semaphore_signal(
            barrier, inc=1, device_id={"row": to_row, "col": other}, device_id_type=MESH
        )
    pl.semaphore_wait(barrier, rows_n + 2)

    step_wins = 4
    step = step_wins * SPAN
    steps = wins // step_wins
    span_cols = step_wins * WIN

    def halo(i, src, dst, to_row, to_col):
        return remote(src, dst, halo_send.at[i], halo_recv.at[i], to_row, to_col)

    labels = [halo(0, reg, reg_b, up, col), halo(1, reg, reg_r, row, other)]
    sides = [
        halo(2, tok.at[SHIFT:WIN, 0:EDGE], tok_r, row, other),
        halo(3, tok.at[0:SHIFT, 0:EDGE], tok_d, up, other),
        halo(4, grad.at[SHIFT:WIN, 0:EDGE], grad_r, row, other),
        halo(5, grad.at[0:SHIFT, 0:EDGE], grad_d, up, other),
    ]
    chunks = []
    for b in range(steps):
        first = b * span_cols + (EDGE if b else 0)
        last = min((b + 1) * span_cols + EDGE, tile_cols)
        chunks.append([
            halo(6 + 2 * b + i, src.at[0:SHIFT, first:last], dst.at[0:SHIFT, first:last], up, col)
            for i, (src, dst) in enumerate(((tok, tok_b), (grad, grad_b)))
        ])
    for copy in labels + chunks[0] + sides + chunks[1]:
        copy.start()

    flat = exact(table[...], table_spread(table.shape[1]))
    for rj in range(WIN):
        span_b[pl.ds(rj, HEADS, stride=WIN), :] = exact(flat, row_spread(rj), NT)
    for cj in range(WIN):
        span_a[pl.ds(cj, HEADS * WIN, stride=WIN), :] = exact(span_b[...], col_spread(cj), NT)
    for h in range(HEADS):
        bias_t[:, h * SPAN : (h + 1) * SPAN] = span_a[h * SPAN : (h + 1) * SPAN, :]
    mask_row = iota((LANES, C), 0) >> 6
    mask_col = iota((LANES, C), 1)
    hmask[...] = (
        (mask_col >= mask_row * HEAD) & (mask_col < (mask_row + 1) * HEAD)
    ).astype(F32).astype(BF16)
    score_acc[...] = jnp.zeros_like(score_acc)
    pack[...] = jnp.zeros_like(pack)

    nt_s[...] = jnp.ones_like(nt_s)
    for cj in range(WIN):
        fold_a[cj * SPAN : (cj + 1) * SPAN, :] = col_spread(cj).astype(BF16)
    for rj in range(WIN):
        fold_b[rj * 128 : (rj + 1) * 128, :] = row_spread(rj).astype(BF16)
    weights = qkvw[...]
    offsets = qkvb[...]
    for i in range(3):
        w_s[i] = weights[:, i * C : (i + 1) * C]
        b_s[i] = offsets[:, i * C : (i + 1) * C]

    for copy in labels:
        copy.wait()

    own = reg[...]
    row_part = jnp.concatenate([own[SHIFT:], reg_b[0:SHIFT, :]], 0)[:, 0:1] >> 2
    col_own = pltpu.roll(own, tile_cols - SHIFT, 1)
    col_right = pltpu.roll(reg_r[...], tile_cols - SHIFT, 1)
    col_part = jnp.where(iota((WIN, tile_cols), 1) < tile_cols - SHIFT, col_own, col_right)[0:1] & 3
    label = (row_part * 4 + col_part).astype(F32)
    spread = jnp.broadcast_to(label[:, None, :], (WIN, WIN, tile_cols)).reshape(SPAN, tile_cols)
    spread = jnp.where(
        (iota((SPAN, tile_cols), 0) & 7) == (iota((SPAN, tile_cols), 1) & 7), spread, 0.0
    )
    pick = ((iota((tile_cols, wins), 0) >> 3) == iota((tile_cols, wins), 1)).astype(F32)
    columns = exact(spread, pick)
    tiled = (iota((SPAN, LANES), 0) == (iota((SPAN, LANES), 1) & (SPAN - 1))).astype(F32)
    lab_row[...] = exact(columns, tiled, TN)
    for w in range(wins):
        lab_col[w] = jnp.broadcast_to(columns[:, w : w + 1], (SPAN, 128))

    def gather_heads(stacked):
        kept = stacked * hmask[...].astype(F32)
        return jnp.sum(kept.reshape(HEADS, SPAN, C), 0)

    small = 4 * BLOCK
    edge = tile_cols - EDGE
    backs = []

    def back(src, dst, to_row, to_col):
        i = len(backs)
        backs.append(remote(src, dst, back_send.at[i], back_recv.at[i], to_row, to_col))
        backs[-1].start()

    for b in range(steps):
        for copy in chunks[b] + (sides if b == steps - 1 else []):
            copy.wait()
        if b + 2 < steps:
            for copy in chunks[b + 2]:
                copy.start()
        at = slice(b * step, (b + 1) * step)
        win_at = slice(b * step_wins, (b + 1) * step_wins)
        cols = slice(b * span_cols, (b + 1) * span_cols)
        near = slice(b * span_cols, min((b + 1) * span_cols + EDGE, tile_cols))

        for main, below, right, diag, target in (
            (tok, tok_b, tok_r, tok_d, unit),
            (grad, grad_b, grad_r, grad_d, gradf),
        ):
            for r in range(WIN):
                if r < SHIFT:
                    part, beyond = main[r + SHIFT, near], right[r]
                else:
                    part, beyond = below[r - SHIFT, near], diag[r - SHIFT]
                wide = part.astype(F32)
                if b == steps - 1:
                    wide = jnp.concatenate([wide, beyond.astype(F32)], 0)
                target[win_at, r] = wide[SHIFT : SHIFT + span_cols].reshape(step_wins, WIN, C)

        x = unit[win_at].reshape(step, C)
        center = jnp.mean(x, -1, keepdims=True)
        x = x - center
        inv = lax.rsqrt(jnp.mean(x * x, -1, keepdims=True) + 1e-05)
        x = x * inv
        unit[win_at] = x.reshape(step_wins, WIN, WIN, C)
        inv_std[at] = inv
        n = (x * gain_ref[...] + offset_ref[...]).astype(BF16)
        nt_s[0:C, at] = n.T
        q_s[at] = ((mul(n, w_s[0]) + b_s[0]) * HEAD ** (-0.5)).astype(BF16)
        k_s[at] = (mul(n, w_s[1]) + b_s[1]).astype(BF16)
        v_s[at] = (mul(n, w_s[2]) + b_s[2]).astype(BF16)
        g = gradf[win_at].reshape(step, C).astype(BF16)
        gb_s[at] = g
        da_s[at] = mul(g, projw[...], NT).astype(BF16)

        @pl.loop(0, step_wins // 2)
        def _(pair_at):
            loaded = []
            for i in range(2):
                w = b * step_wins + pair_at * 2 + i
                at = pl.ds(pl.multiple_of(w * SPAN, SPAN), SPAN)
                same = lab_col[w][:, 0:1] == lab_row[pl.ds(w, 1), :]
                loaded.append((at, q_s[at], k_s[at], v_s[at], da_s[at], same))
            heads = hmask[...]
            bias = bias_t[...]
            total = score_acc[...]
            for at, q, k, v, da, same in loaded:
                qm = jnp.concatenate([q] * HEADS, 0) * heads
                dam = jnp.concatenate([da] * HEADS, 0) * heads
                scores = jnp.where(same, mul(k, qm, NT) + bias, MASKED)
                e = jnp.exp(scores - jnp.max(scores, 0, keepdims=True))
                p = e * (1.0 / jnp.sum(e, 0, keepdims=True))
                p_low = p.astype(BF16)
                att[at] = gather_heads(mul(p_low, v, TN)).astype(BF16)
                dp = mul(v, dam, NT)
                ds = p * (dp - jnp.sum(p * dp, 0, keepdims=True))
                total += ds
                ds_low = ds.astype(BF16)
                dq_s[at] = (gather_heads(mul(ds_low, k, TN)) * HEAD ** (-0.5)).astype(BF16)
                dk_s[at] = mul(ds_low, qm).astype(BF16)
                dv_s[at] = mul(p_low, dam).astype(BF16)
            score_acc[...] = total

        x = unit[win_at].reshape(step, C)
        dn = mul(dq_s[at], w_s[0], NT) + mul(dk_s[at], w_s[1], NT) + mul(dv_s[at], w_s[2], NT)
        pack[small + 3 : small + 4, 0:C] += jnp.sum(dn * x, 0, keepdims=True)
        pack[small + 4 : small + 5, 0:C] += jnp.sum(dn, 0, keepdims=True)
        g = dn * gain_ref[...]
        dx = inv_std[at] * (
            g - jnp.mean(g, -1, keepdims=True) - x * jnp.mean(g * x, -1, keepdims=True)
        )
        out = (gradf[win_at].reshape(step, C) + dx).reshape(step_wins, WIN, WIN, C)
        for r in range(WIN):
            frame_low[r, cols] = out[:, r].reshape(span_cols, C).astype(BF16)
        back(frame_low.at[SHIFT:WIN, cols], back_u.at[0:SHIFT, cols], down, col)
        if b == steps - 1:
            back(frame_low.at[0:SHIFT, edge:tile_cols], back_l, row, other)
            back(frame_low.at[SHIFT:WIN, edge:tile_cols], back_ul, down, other)

    for i, part in enumerate((dq_s, dk_s, dv_s)):
        pack[i * BLOCK : (i + 1) * BLOCK, 0:C] = mul(nt_s[...], part[...])[0:BLOCK]
    pack[3 * BLOCK : 3 * BLOCK + C, 0:C] = mul(att[...], gb_s[...], TN)
    for h in range(HEADS):
        span_a[h * SPAN : (h + 1) * SPAN, :] = score_acc[:, h * SPAN : (h + 1) * SPAN]
    wide = jnp.concatenate(
        [span_a[pl.ds(cj, HEADS * WIN, stride=WIN), :] for cj in range(WIN)], 1
    )
    span_b[...] = split_mul(wide, fold_a[...])
    wide = jnp.concatenate(
        [span_b[pl.ds(rj, HEADS, stride=WIN), :] for rj in range(WIN)], 1
    )
    flat_sum = split_mul(wide, fold_b[...])
    pack[small + 8 : small + 8 + HEADS, :] = flat_sum
    pack_low[...] = pack[...].astype(BF16)

    pair = remote(
        pack_low.at[pl.ds(pl.multiple_of(other * half, 16), half)], pair_in,
        pair_sem.at[0], pair_sem.at[1], row, other,
    )
    pair.start()
    pair.wait()
    mine = pl.ds(pl.multiple_of(col * half, 16), half)
    half_low[...] = (pack[mine] + pair_in[...].astype(F32)).astype(BF16)

    def part_copy(k):
        peer = lax.rem(row + k, rows_n)
        return remote(
            half_low.at[pl.ds(pl.multiple_of(peer * chunk, 16), chunk)], part_in.at[k],
            part_send.at[k], part_recv.at[k], peer, col,
        )

    @pl.loop(1, rows_n)
    def _(k):
        part_copy(k).start()

    for copy in backs:
        copy.wait()
    for r in range(WIN):
        if r < SHIFT:
            left_part, main_part = back_ul[r], back_u[r]
        else:
            left_part, main_part = back_l[r - SHIFT], frame_low[r - SHIFT]
        wide = jnp.concatenate([left_part.astype(F32), main_part.astype(F32)], 0)
        d_tok[r] = wide[EDGE - SHIFT : EDGE - SHIFT + tile_cols].astype(BF16)

    def add_part(k, total):
        part_copy(k).wait()
        return total + part_in[k].astype(F32)

    my_chunk = pl.ds(pl.multiple_of(row * chunk, 16), chunk)
    total = lax.fori_loop(1, rows_n, add_part, half_low[my_chunk].astype(F32))
    own_chunk = result.at[col, my_chunk]
    own_chunk[...] = total.astype(BF16)

    def all_copy(k):
        return remote(
            own_chunk, own_chunk, all_send.at[k], all_recv.at[k],
            lax.rem(row + k, rows_n), col,
        )

    def forward(k):
        source = lax.rem(row + rows_n - k, rows_n)
        piece = result.at[col, pl.ds(pl.multiple_of(source * chunk, 16), chunk)]
        return remote(piece, piece, fwd_send.at[k], fwd_recv.at[k], row, other)

    @pl.loop(1, rows_n)
    def _(k):
        all_copy(k).start()

    forward(0).start()

    @pl.loop(1, rows_n)
    def _(k):
        all_copy(k).wait()
        forward(k).start()

    @pl.loop(0, rows_n)
    def _(k):
        forward(k).wait()

    pack[0:half] = result[0].astype(F32) * out_scale
    pack[half : 2 * half] = result[1].astype(F32) * out_scale
    d_qkvw[...] = jnp.concatenate(
        [pack[i * BLOCK : i * BLOCK + C, 0:C] for i in range(3)], 1
    )
    d_qkvb[...] = jnp.concatenate(
        [pack[i * BLOCK + C : i * BLOCK + C + 1, 0:C] for i in range(3)], 1
    )
    d_projw[...] = pack[3 * BLOCK : 3 * BLOCK + C, 0:C]
    d_gain[...] = pack[small + 3 : small + 4, 0:C]
    d_offset[...] = pack[small + 4 : small + 5, 0:C]
    entries = table_spread(d_table.shape[1])
    d_table[...] = exact(pack[small + 8 : small + 8 + HEADS, :], entries, NT)


def on_device(
    tokens, grad_out, regions, ln_gain, ln_offset, qkv_weight, qkv_bias, proj_weight, bias_table
):
    rows_n, cols_n = lax.axis_size("row"), lax.axis_size("col")
    tile_cols = tokens.shape[1]
    wins = tile_cols // WIN
    count = wins * SPAN
    steps = wins // 4
    unit_rows = 2 * 16 * rows_n
    needed = 4 * BLOCK + 16
    rows_total = -(-needed // unit_rows) * unit_rows
    half = rows_total // 2
    chunk = half // rows_n
    total_tokens = tokens.shape[0] * tile_cols * rows_n * cols_n
    vmem = pltpu.VMEM
    halo = [
        vmem((SHIFT, tile_cols, C), BF16),
        vmem((SHIFT, EDGE, C), BF16),
        vmem((SHIFT, EDGE, C), BF16),
    ]
    flat_low = vmem((count, C), BF16)
    whole = pl.BlockSpec(memory_space=pltpu.VMEM)
    dma = pltpu.SemaphoreType.DMA
    outs = pl.pallas_call(
        functools.partial(body, rows_n, cols_n, rows_total, total_tokens ** (-0.5)),
        out_shape=(
            jax.ShapeDtypeStruct(tokens.shape, BF16),
            jax.ShapeDtypeStruct((C, 3 * C), F32),
            jax.ShapeDtypeStruct((1, 3 * C), F32),
            jax.ShapeDtypeStruct((C, C), F32),
            jax.ShapeDtypeStruct((HEADS, bias_table.shape[0]), F32),
            jax.ShapeDtypeStruct((1, C), F32),
            jax.ShapeDtypeStruct((1, C), F32),
        ),
        in_specs=[whole] * 9,
        out_specs=(whole,) * 7,
        scratch_shapes=halo + halo + [
            vmem(regions.shape, jnp.int32),
            vmem(regions.shape, jnp.int32),
            vmem((wins, WIN, WIN, C), F32),
            vmem((count, 1), F32),
            vmem((wins, WIN, WIN, C), F32),
            vmem((192, count), BF16),
        ] + [flat_low] * 9 + [
            vmem((3, C, C), BF16),
            vmem((3, 1, C), F32),
            vmem((SPAN, LANES), F32),
            vmem((HEADS * SPAN, SPAN), F32),
            vmem((HEADS * WIN, 128), F32),
            vmem((LANES, C), BF16),
            vmem((wins, SPAN, 128), F32),
            vmem((wins, LANES), F32),
            vmem((SPAN, LANES), F32),
            vmem((WIN * SPAN, 128), BF16),
            vmem((WIN * 128, 256), BF16),
            vmem((WIN, tile_cols, C), BF16),
        ] + halo + [
            vmem((rows_total, 256), F32),
            vmem((rows_total, 256), BF16),
            vmem((half, 256), BF16),
            vmem((half, 256), BF16),
            vmem((rows_n, chunk, 256), BF16),
            vmem((2, half, 256), BF16),
            dma((6 + 2 * steps,)), dma((6 + 2 * steps,)),
            dma((steps + 2,)), dma((steps + 2,)), dma((2,)),
            dma((rows_n,)), dma((rows_n,)), dma((rows_n,)), dma((rows_n,)),
            dma((rows_n,)), dma((rows_n,)),
        ],
        compiler_params=pltpu.CompilerParams(
            collective_id=0, has_side_effects=True, vmem_limit_bytes=48 * 1024 * 1024
        ),
    )(
        tokens, grad_out, regions, ln_gain.reshape(1, C), ln_offset.reshape(1, C), qkv_weight,
        qkv_bias.reshape(1, 3 * C), proj_weight, bias_table.T,
    )
    d_tokens, d_qkvw, d_qkvb, d_projw, d_table, d_gain, d_offset = outs
    return (
        d_tokens,
        d_qkvw,
        d_qkvb.reshape(3 * C),
        d_projw,
        d_table.T,
        d_gain.reshape(C),
        d_offset.reshape(C),
    )


def solution(mesh):
    placed = (
        P(("grp", "row"), "col", None),
        P(("grp", "row"), "col", None),
        P(("grp", "row"), "col"),
        P(),
        P(),
        P(),
        P(),
        P(),
        P(),
    )
    return jax.shard_map(
        on_device,
        mesh=mesh,
        in_specs=placed,
        out_specs=(
            P(("grp", "row"), "col", None),
            P("grp", None),
            P("grp"),
            P("grp", None),
            P("grp", None),
            P("grp"),
            P("grp"),
        ),
        check_vma=False,
    )
```

time: 70.7 us -> 53.6 us (0.76)
  Pallas kernels: 59.7 us -> 44.9 us
  local copies, waits for them, and re-layouts: 9.96 us -> 7.11 us
    pallas_call x1, Pallas kernels: 59.7 us -> 44.9 us  [on_device(): pl.pallas_call(functools.partial(body, rows_n, cols_n, rows_total, total_...]
    reshape x4 -> x1, local copies, waits for them, and re-layouts: 2.68 us -> 0.01 us  [on_device(): qkv_bias.reshape(1, 3 * C)]
    unnamed x22 -> x24, local copies, waits for them, and re-layouts: 6.72 us -> 7.11 us
where the time goes in v2:
time: 53.6 us; the launch traced here: 53.4 us
  Pallas kernels  44.9 us (84%)
  local copies, waits for them, and re-layouts  7.11 us (13%)
  between operations  0.73 us (1%)
  other arithmetic  0.6 us (1%)
    pallas_call x1, Pallas kernels, on_device(): pl.pallas_call(functools.partial(body, rows_n, cols_n, rows_total, total_...  44.9 us
    unnamed x24, local copies, waits for them, and re-layouts  7.11 us

profile of v2, /device:TPU:0, one launch (start us, length us, event | category | flops | bytes accessed | tf_op | source)
XLA Modules:
  0.0 53.4 jit_solution(16019020213545107811)
XLA Ops:
  0.6 0.0 copy-start.7
  0.6 0.7 %copy-done.7 = f32[540]{0:T(1024)S(1)} copy-done((f32[540]{0:T(1024)S(1)}, f32[540]{0:T(1024)}, u32[]{:S(2)}) %copy-start.7) | copy-done | bytes 2184
  1.3 0.0 copy-start.6
  1.3 1.3 %copy.16.tok = bf16[8,128,180]{2,1,0:T(8,128)(2,1)S(1)} copy(bf16[8,128,180]{1,0,2:T(8,128)(2,1)} %param.9) | data formatting | bytes 737280 | tf_op args[0]
  2.6 0.0 copy-done.6
  2.6 0.0 copy-start
  2.6 0.0 copy-start.1
  2.7 0.0 copy-start.2
  2.7 0.0 copy-start.3
  2.7 0.0 copy-start.4
  2.7 0.0 copy-start.5
  2.7 0.3 copy.17.grad
  3.0 0.6 %copy-done = bf16[180,540]{1,0:T(8,128)(2,1)S(1)} copy-done((bf16[180,540]{1,0:T(8,128)(2,1)S(1)}, bf16[180,540]{1,0:T(8,128)(2,1)}, u32[]{:S(2)}) %copy-start) | copy-done | bytes 194424
  3.6 0.1 copy-done.1
  3.6 0.0 copy-done.2
  3.6 0.0 copy-done.3
  3.7 0.0 copy-done.4
  3.7 0.0 copy-done.5
  3.7 44.9 %shard_map.144 = (bf16[8,128,180]{2,1,0:T(8,128)(2,1)S(1)}, f32[180,540]{1,0:T(8,128)S(1)}, f32[1,540]{1,0:T(1,128)S(1)}, f32[180,180]{1,0:T(8,128)S(1)}, f32[6,...) custom-call(bf16[8,128,180]{2,1,0:T(8,128)(2,1)S(1)} %copy.16.tok, ...), custom_call_target="tpu_custom_call" | custom-call | tf_op jit(solution)/shard_map/pallas_call | solution.py:401
  48.6 1.0 %copy.18 = bf16[8,128,180]{1,0,2:T(8,128)(2,1)} copy(bf16[8,128,180]{2,1,0:T(8,128)(2,1)S(1)} %get-tuple-element.21) | data formatting | bytes 737280
  49.6 0.6 %reduce = f32[540]{0:T(1024)} reduce(f32[1,540]{1,0:T(1,128)S(1)} %get-tuple-element.16, f32[]{:T(128)} %constant.3), dimensions={0}, to_apply=%get-tuple-element.16.reduce_sub_computation | reduce | bytes 4324 | tf_op jit(solution)/shard_map/pallas_call | solution.py:401
  50.2 0.8 %copy.24 = f32[180,540]{1,0:T(8,128)} copy(f32[180,540]{1,0:T(8,128)S(1)} %get-tuple-element.36) | data formatting | bytes 777600
  51.0 0.7 %copy.25 = f32[180,180]{1,0:T(8,128)} copy(f32[180,180]{1,0:T(8,128)S(1)} %get-tuple-element.38) | data formatting | bytes 259200
  51.6 0.6 %copy.26 = f32[225,6]{0,1:T(8,128)} copy(f32[225,6]{0,1:T(8,128)S(1)} %bitcast.7) | data formatting | bytes 10800
  52.2 0.6 %copy.27 = f32[180]{0:T(256)} copy(f32[180]{0:T(256)S(1)} %bitcast.11) | data formatting | bytes 1440
  52.8 0.6 %copy.28 = f32[180]{0:T(256)} copy(f32[180]{0:T(256)S(1)} %bitcast.10) | data formatting | bytes 1440
  (1 shorter events, 0.0 us)
Async XLA Ops:
  0.6 0.7 %copy-start.7 = (f32[540]{0:T(1024)S(1)}, f32[540]{0:T(1024)}, u32[]{:S(2)}) copy-start(f32[540]{0:T(1024)} %param.15) | copy-start | bytes 6484
  1.3 1.3 %copy-start.6 = (bf16[8,128,180]{1,0,2:T(8,128)(2,1)S(1)}, bf16[8,128,180]{1,0,2:T(8,128)(2,1)}, u32[]{:S(2)}) copy-start(bf16[8,128,180]{1,0,2:T(8,128)(2,1)} %param.10) | copy-start | bytes 1105924
  2.6 0.9 %copy-start = (bf16[180,540]{1,0:T(8,128)(2,1)S(1)}, bf16[180,540]{1,0:T(8,128)(2,1)}, u32[]{:S(2)}) copy-start(bf16[180,540]{1,0:T(8,128)(2,1)} %qkvw.1) | copy-start | bytes 583204
  2.6 1.0 %copy-start.1 = (bf16[180,180]{1,0:T(8,128)(2,1)S(1)}, bf16[180,180]{1,0:T(8,128)(2,1)}, u32[]{:S(2)}) copy-start(bf16[180,180]{1,0:T(8,128)(2,1)} %projw.1) | copy-start | bytes 194404
  2.7 1.0 %copy-start.2 = (f32[225,6]{0,1:T(8,128)S(1)}, f32[225,6]{0,1:T(8,128)}, u32[]{:S(2)}) copy-start(f32[225,6]{0,1:T(8,128)} %param.17) | copy-start | bytes 16204
  2.7 1.0 %copy-start.3 = (s32[8,128]{1,0:T(8,128)S(1)}, s32[8,128]{1,0:T(8,128)}, u32[]{:S(2)}) copy-start(s32[8,128]{1,0:T(8,128)} %reg.1) | copy-start | bytes 12292
  2.7 1.0 %copy-start.4 = (f32[180]{0:T(256)S(1)}, f32[180]{0:T(256)}, u32[]{:S(2)}) copy-start(f32[180]{0:T(256)} %param.12) | copy-start | bytes 2164
  2.7 1.0 %copy-start.5 = (f32[180]{0:T(256)S(1)}, f32[180]{0:T(256)}, u32[]{:S(2)}) copy-start(f32[180]{0:T(256)} %param.13) | copy-start | bytes 2164

commit v3 on v2

--- a/solution.py
+++ b/solution.py
@@ -69,7 +69,7 @@
     rows_n, cols_n, rows_total, out_scale,
     tok, grad, reg, gain_ref, offset_ref, qkvw, qkvb, projw, table,
     d_tok, d_qkvw, d_qkvb, d_projw, d_table, d_gain, d_offset,
-    tok_b, tok_r, tok_d, grad_b, grad_r, grad_d, reg_b, reg_r,
+    tok_b, tok_r, tok_d, grad_b, grad_r, grad_d, tok_a, grad_a, reg_b, reg_r, reg_a,
     unit, inv_std, gradf, nt_s, q_s, k_s, v_s, da_s, gb_s, att, dq_s, dk_s, dv_s,
     w_s, b_s, bias_t, span_a, span_b, hmask, lab_col, lab_row, score_acc,
     fold_a, fold_b, frame_low, back_u, back_l, back_ul,
@@ -117,22 +117,36 @@
     def halo(i, src, dst, to_row, to_col):
         return remote(src, dst, halo_send.at[i], halo_recv.at[i], to_row, to_col)
 
-    labels = [halo(0, reg, reg_b, up, col), halo(1, reg, reg_r, row, other)]
+    middle = steps // 2
+    labels = [
+        halo(0, reg, reg_b, up, col),
+        halo(1, reg, reg_r, row, other),
+        halo(2, reg, reg_a, down, col),
+    ]
     sides = [
-        halo(2, tok.at[SHIFT:WIN, 0:EDGE], tok_r, row, other),
-        halo(3, tok.at[0:SHIFT, 0:EDGE], tok_d, up, other),
-        halo(4, grad.at[SHIFT:WIN, 0:EDGE], grad_r, row, other),
-        halo(5, grad.at[0:SHIFT, 0:EDGE], grad_d, up, other),
+        halo(3, tok.at[0:SHIFT, 0:EDGE], tok_r, row, other),
+        halo(4, tok.at[SHIFT:WIN, 0:EDGE], tok_d, down, other),
+        halo(5, grad.at[0:SHIFT, 0:EDGE], grad_r, row, other),
+        halo(6, grad.at[SHIFT:WIN, 0:EDGE], grad_d, down, other),
     ]
     chunks = []
     for b in range(steps):
-        first = b * span_cols + (EDGE if b else 0)
+        first = b * span_cols + (EDGE if b % middle else 0)
         last = min((b + 1) * span_cols + EDGE, tile_cols)
+        if b < middle:
+            ends = ((tok, tok_b), (grad, grad_b))
+            rows, to_row = slice(0, SHIFT), up
+        else:
+            ends = ((tok, tok_a), (grad, grad_a))
+            rows, to_row = slice(SHIFT, WIN), down
         chunks.append([
-            halo(6 + 2 * b + i, src.at[0:SHIFT, first:last], dst.at[0:SHIFT, first:last], up, col)
-            for i, (src, dst) in enumerate(((tok, tok_b), (grad, grad_b)))
+            halo(
+                7 + 2 * b + i, src.at[rows, first:last], dst.at[0:SHIFT, first:last], to_row, col
+            )
+            for i, (src, dst) in enumerate(ends)
         ])
-    for copy in labels + chunks[0] + sides + chunks[1]:
+    order = [b + side * middle for b in range(middle) for side in range(2)]
+    for copy in labels + chunks[order[0]] + chunks[order[1]] + sides:
         copy.start()
 
     flat = exact(table[...], table_spread(table.shape[1]))
@@ -165,7 +179,13 @@
         copy.wait()
 
     own = reg[...]
-    row_part = jnp.concatenate([own[SHIFT:], reg_b[0:SHIFT, :]], 0)[:, 0:1] >> 2
+    row_left = jnp.concatenate([own[SHIFT:], reg_b[0:SHIFT, :]], 0)[:, 0:1] >> 2
+    row_right = jnp.concatenate([reg_a[SHIFT:WIN, :], own[0:SHIFT]], 0)[:, 0:1] >> 2
+    row_part = jnp.where(
+        iota((WIN, tile_cols), 1) < middle * span_cols,
+        jnp.broadcast_to(row_left, (WIN, tile_cols)),
+        jnp.broadcast_to(row_right, (WIN, tile_cols)),
+    )
     col_own = pltpu.roll(own, tile_cols - SHIFT, 1)
     col_right = pltpu.roll(reg_r[...], tile_cols - SHIFT, 1)
     col_part = jnp.where(iota((WIN, tile_cols), 1) < tile_cols - SHIFT, col_own, col_right)[0:1] & 3
@@ -187,6 +207,7 @@
 
     small = 4 * BLOCK
     edge = tile_cols - EDGE
+    cut = middle * span_cols
     backs = []
 
     def back(src, dst, to_row, to_col):
@@ -194,28 +215,29 @@
         backs.append(remote(src, dst, back_send.at[i], back_recv.at[i], to_row, to_col))
         backs[-1].start()
 
-    for b in range(steps):
+    for place, b in enumerate(order):
         for copy in chunks[b] + (sides if b == steps - 1 else []):
             copy.wait()
-        if b + 2 < steps:
-            for copy in chunks[b + 2]:
+        if place + 2 < steps:
+            for copy in chunks[order[place + 2]]:
                 copy.start()
         at = slice(b * step, (b + 1) * step)
         win_at = slice(b * step_wins, (b + 1) * step_wins)
         cols = slice(b * span_cols, (b + 1) * span_cols)
         near = slice(b * span_cols, min((b + 1) * span_cols + EDGE, tile_cols))
 
-        for main, below, right, diag, target in (
-            (tok, tok_b, tok_r, tok_d, unit),
-            (grad, grad_b, grad_r, grad_d, gradf),
+        for main, below, above, right, diag, target in (
+            (tok, tok_b, tok_a, tok_r, tok_d, unit),
+            (grad, grad_b, grad_a, grad_r, grad_d, gradf),
         ):
             for r in range(WIN):
-                if r < SHIFT:
-                    part, beyond = main[r + SHIFT, near], right[r]
+                if b < middle:
+                    part = main[r + SHIFT, near] if r < SHIFT else below[r - SHIFT, near]
                 else:
-                    part, beyond = below[r - SHIFT, near], diag[r - SHIFT]
+                    part = above[r, near] if r < SHIFT else main[r - SHIFT, near]
                 wide = part.astype(F32)
                 if b == steps - 1:
+                    beyond = diag[r] if r < SHIFT else right[r - SHIFT]
                     wide = jnp.concatenate([wide, beyond.astype(F32)], 0)
                 target[win_at, r] = wide[SHIFT : SHIFT + span_cols].reshape(step_wins, WIN, C)
 
@@ -274,10 +296,13 @@
         out = (gradf[win_at].reshape(step, C) + dx).reshape(step_wins, WIN, WIN, C)
         for r in range(WIN):
             frame_low[r, cols] = out[:, r].reshape(span_cols, C).astype(BF16)
-        back(frame_low.at[SHIFT:WIN, cols], back_u.at[0:SHIFT, cols], down, col)
+        if b < middle:
+            back(frame_low.at[SHIFT:WIN, cols], back_u.at[0:SHIFT, cols], down, col)
+        else:
+            back(frame_low.at[0:SHIFT, cols], back_u.at[0:SHIFT, cols], up, col)
         if b == steps - 1:
-            back(frame_low.at[0:SHIFT, edge:tile_cols], back_l, row, other)
-            back(frame_low.at[SHIFT:WIN, edge:tile_cols], back_ul, down, other)
+            back(frame_low.at[SHIFT:WIN, edge:tile_cols], back_l, row, other)
+            back(frame_low.at[0:SHIFT, edge:tile_cols], back_ul, up, other)
 
     for i, part in enumerate((dq_s, dk_s, dv_s)):
         pack[i * BLOCK : (i + 1) * BLOCK, 0:C] = mul(nt_s[...], part[...])[0:BLOCK]
@@ -319,10 +344,12 @@
         copy.wait()
     for r in range(WIN):
         if r < SHIFT:
-            left_part, main_part = back_ul[r], back_u[r]
+            pieces = (back_l[r], back_u[r, 0:cut], frame_low[r + SHIFT, cut:tile_cols])
         else:
-            left_part, main_part = back_l[r - SHIFT], frame_low[r - SHIFT]
-        wide = jnp.concatenate([left_part.astype(F32), main_part.astype(F32)], 0)
+            pieces = (
+                back_ul[r - SHIFT], frame_low[r - SHIFT, 0:cut], back_u[r - SHIFT, cut:tile_cols]
+            )
+        wide = jnp.concatenate([piece.astype(F32) for piece in pieces], 0)
         d_tok[r] = wide[EDGE - SHIFT : EDGE - SHIFT + tile_cols].astype(BF16)
 
     def add_part(k, total):
@@ -412,6 +439,9 @@
         in_specs=[whole] * 9,
         out_specs=(whole,) * 7,
         scratch_shapes=halo + halo + [
+            halo[0],
+            halo[0],
+            vmem(regions.shape, jnp.int32),
             vmem(regions.shape, jnp.int32),
             vmem(regions.shape, jnp.int32),
             vmem((wins, WIN, WIN, C), F32),
@@ -438,7 +468,7 @@
             vmem((half, 256), BF16),
             vmem((rows_n, chunk, 256), BF16),
             vmem((2, half, 256), BF16),
-            dma((6 + 2 * steps,)), dma((6 + 2 * steps,)),
+            dma((7 + 2 * steps,)), dma((7 + 2 * steps,)),
             dma((steps + 2,)), dma((steps + 2,)), dma((2,)),
             dma((rows_n,)), dma((rows_n,)), dma((rows_n,)), dma((rows_n,)),
             dma((rows_n,)), dma((rows_n,)),

time: 53.6 us -> 56.7 us (1.058)
  Pallas kernels: 44.9 us -> 48.1 us
    pallas_call x1, Pallas kernels: 44.9 us -> 48.1 us  [on_device(): pl.pallas_call(functools.partial(body, rows_n, cols_n, rows_total, total_...]
where the time goes in v3:
time: 56.7 us; the launch traced here: 56.5 us
  Pallas kernels  48.1 us (85%)
  local copies, waits for them, and re-layouts  7.11 us (13%)
  between operations  0.73 us (1%)
  other arithmetic  0.6 us (1%)
    pallas_call x1, Pallas kernels, on_device(): pl.pallas_call(functools.partial(body, rows_n, cols_n, rows_total, total_...  48.1 us
    unnamed x24, local copies, waits for them, and re-layouts  7.11 us

profile of v3, /device:TPU:0, one launch (start us, length us, event | category | flops | bytes accessed | tf_op | source)
XLA Modules:
  0.0 56.5 jit_solution(9512269514391195003)
XLA Ops:
  0.6 0.0 copy-start.7
  0.6 0.7 %copy-done.7 = f32[540]{0:T(1024)S(1)} copy-done((f32[540]{0:T(1024)S(1)}, f32[540]{0:T(1024)}, u32[]{:S(2)}) %copy-start.7) | copy-done | bytes 2184
  1.3 0.0 copy-start.6
  1.3 1.3 %copy.16.tok = bf16[8,128,180]{2,1,0:T(8,128)(2,1)S(1)} copy(bf16[8,128,180]{1,0,2:T(8,128)(2,1)} %param.9) | data formatting | bytes 737280 | tf_op args[0]
  2.6 0.0 copy-done.6
  2.6 0.0 copy-start
  2.6 0.0 copy-start.1
  2.7 0.0 copy-start.2
  2.7 0.0 copy-start.3
  2.7 0.0 copy-start.4
  2.7 0.0 copy-start.5
  2.7 0.3 copy.17.grad
  3.0 0.6 %copy-done = bf16[180,540]{1,0:T(8,128)(2,1)S(1)} copy-done((bf16[180,540]{1,0:T(8,128)(2,1)S(1)}, bf16[180,540]{1,0:T(8,128)(2,1)}, u32[]{:S(2)}) %copy-start) | copy-done | bytes 194424
  3.6 0.1 copy-done.1
  3.6 0.0 copy-done.2
  3.6 0.0 copy-done.3
  3.7 0.0 copy-done.4
  3.7 0.0 copy-done.5
  3.7 48.1 %shard_map.144 = (bf16[8,128,180]{2,1,0:T(8,128)(2,1)S(1)}, f32[180,540]{1,0:T(8,128)S(1)}, f32[1,540]{1,0:T(1,128)S(1)}, f32[180,180]{1,0:T(8,128)S(1)}, f32[6,...) custom-call(bf16[8,128,180]{2,1,0:T(8,128)(2,1)S(1)} %copy.16.tok, ...), custom_call_target="tpu_custom_call" | custom-call | tf_op jit(solution)/shard_map/pallas_call | solution.py:428
  51.7 1.0 %copy.18 = bf16[8,128,180]{1,0,2:T(8,128)(2,1)} copy(bf16[8,128,180]{2,1,0:T(8,128)(2,1)S(1)} %get-tuple-element.21) | data formatting | bytes 737280
  52.7 0.6 %reduce = f32[540]{0:T(1024)} reduce(f32[1,540]{1,0:T(1,128)S(1)} %get-tuple-element.16, f32[]{:T(128)} %constant.3), dimensions={0}, to_apply=%get-tuple-element.16.reduce_sub_computation | reduce | bytes 4324 | tf_op jit(solution)/shard_map/pallas_call | solution.py:428
  53.3 0.8 %copy.24 = f32[180,540]{1,0:T(8,128)} copy(f32[180,540]{1,0:T(8,128)S(1)} %get-tuple-element.36) | data formatting | bytes 777600
  54.1 0.7 %copy.25 = f32[180,180]{1,0:T(8,128)} copy(f32[180,180]{1,0:T(8,128)S(1)} %get-tuple-element.38) | data formatting | bytes 259200
  54.8 0.6 %copy.26 = f32[225,6]{0,1:T(8,128)} copy(f32[225,6]{0,1:T(8,128)S(1)} %bitcast.7) | data formatting | bytes 10800
  55.4 0.6 copy.27
  55.9 0.6 copy.28
  (1 shorter events, 0.0 us)
Async XLA Ops:
  0.6 0.7 %copy-start.7 = (f32[540]{0:T(1024)S(1)}, f32[540]{0:T(1024)}, u32[]{:S(2)}) copy-start(f32[540]{0:T(1024)} %param.15) | copy-start | bytes 6484
  1.3 1.3 %copy-start.6 = (bf16[8,128,180]{1,0,2:T(8,128)(2,1)S(1)}, bf16[8,128,180]{1,0,2:T(8,128)(2,1)}, u32[]{:S(2)}) copy-start(bf16[8,128,180]{1,0,2:T(8,128)(2,1)} %param.10) | copy-start | bytes 1105924
  2.6 0.9 %copy-start = (bf16[180,540]{1,0:T(8,128)(2,1)S(1)}, bf16[180,540]{1,0:T(8,128)(2,1)}, u32[]{:S(2)}) copy-start(bf16[180,540]{1,0:T(8,128)(2,1)} %qkvw.1) | copy-start | bytes 583204
  2.6 1.0 %copy-start.1 = (bf16[180,180]{1,0:T(8,128)(2,1)S(1)}, bf16[180,180]{1,0:T(8,128)(2,1)}, u32[]{:S(2)}) copy-start(bf16[180,180]{1,0:T(8,128)(2,1)} %projw.1) | copy-start | bytes 194404
  2.7 1.0 %copy-start.2 = (f32[225,6]{0,1:T(8,128)S(1)}, f32[225,6]{0,1:T(8,128)}, u32[]{:S(2)}) copy-start(f32[225,6]{0,1:T(8,128)} %param.17) | copy-start | bytes 16204
  2.7 1.0 %copy-start.3 = (s32[8,128]{1,0:T(8,128)S(1)}, s32[8,128]{1,0:T(8,128)}, u32[]{:S(2)}) copy-start(s32[8,128]{1,0:T(8,128)} %reg.1) | copy-start | bytes 12292
  2.7 1.0 %copy-start.4 = (f32[180]{0:T(256)S(1)}, f32[180]{0:T(256)}, u32[]{:S(2)}) copy-start(f32[180]{0:T(256)} %param.12) | copy-start | bytes 2164
  2.7 1.0 %copy-start.5 = (f32[180]{0:T(256)S(1)}, f32[180]{0:T(256)}, u32[]{:S(2)}) copy-start(f32[180]{0:T(256)} %param.13) | copy-start | bytes 2164

commit v4 on v2

--- a/solution.py
+++ b/solution.py
@@ -67,12 +67,12 @@
 
 def body(
     rows_n, cols_n, rows_total, out_scale,
-    tok, grad, reg, gain_ref, offset_ref, qkvw, qkvb, projw, table,
+    both, reg, gain_ref, offset_ref, qkvw, qkvb, projw, table,
     d_tok, d_qkvw, d_qkvb, d_projw, d_table, d_gain, d_offset,
-    tok_b, tok_r, tok_d, grad_b, grad_r, grad_d, reg_b, reg_r,
+    both_b, both_r, both_d, reg_b, reg_r,
     unit, inv_std, gradf, nt_s, q_s, k_s, v_s, da_s, gb_s, att, dq_s, dk_s, dv_s,
     w_s, b_s, bias_t, span_a, span_b, hmask, lab_col, lab_row, score_acc,
-    fold_a, fold_b, frame_low, back_u, back_l, back_ul,
+    fold_a, fold_b, frame_low, frame_two, back_u, back_l, back_ul,
     pack, pack_low, pair_in, half_low, part_in, result,
     halo_send, halo_recv, back_send, back_recv, pair_sem,
     part_send, part_recv, all_send, all_recv, fwd_send, fwd_recv,
@@ -82,7 +82,7 @@
     up = lax.rem(row + rows_n - 1, rows_n)
     down = lax.rem(row + 1, rows_n)
     other = lax.rem(col + 1, cols_n)
-    tile_cols = tok.shape[1]
+    tile_cols = both.shape[1]
     wins = tile_cols // WIN
     count = wins * SPAN
     half = rows_total // 2
@@ -119,19 +119,15 @@
 
     labels = [halo(0, reg, reg_b, up, col), halo(1, reg, reg_r, row, other)]
     sides = [
-        halo(2, tok.at[SHIFT:WIN, 0:EDGE], tok_r, row, other),
-        halo(3, tok.at[0:SHIFT, 0:EDGE], tok_d, up, other),
-        halo(4, grad.at[SHIFT:WIN, 0:EDGE], grad_r, row, other),
-        halo(5, grad.at[0:SHIFT, 0:EDGE], grad_d, up, other),
+        halo(2, both.at[SHIFT:WIN, 0:EDGE], both_r, row, other),
+        halo(3, both.at[0:SHIFT, 0:EDGE], both_d, up, other),
     ]
     chunks = []
     for b in range(steps):
         first = b * span_cols + (EDGE if b else 0)
         last = min((b + 1) * span_cols + EDGE, tile_cols)
-        chunks.append([
-            halo(6 + 2 * b + i, src.at[0:SHIFT, first:last], dst.at[0:SHIFT, first:last], up, col)
-            for i, (src, dst) in enumerate(((tok, tok_b), (grad, grad_b)))
-        ])
+        src, dst = both.at[0:SHIFT, first:last], both_b.at[0:SHIFT, first:last]
+        chunks.append([halo(4 + b, src, dst, up, col)])
     for copy in labels + chunks[0] + sides + chunks[1]:
         copy.start()
 
@@ -205,19 +201,17 @@
         cols = slice(b * span_cols, (b + 1) * span_cols)
         near = slice(b * span_cols, min((b + 1) * span_cols + EDGE, tile_cols))
 
-        for main, below, right, diag, target in (
-            (tok, tok_b, tok_r, tok_d, unit),
-            (grad, grad_b, grad_r, grad_d, gradf),
-        ):
-            for r in range(WIN):
-                if r < SHIFT:
-                    part, beyond = main[r + SHIFT, near], right[r]
-                else:
-                    part, beyond = below[r - SHIFT, near], diag[r - SHIFT]
-                wide = part.astype(F32)
-                if b == steps - 1:
-                    wide = jnp.concatenate([wide, beyond.astype(F32)], 0)
-                target[win_at, r] = wide[SHIFT : SHIFT + span_cols].reshape(step_wins, WIN, C)
+        for r in range(WIN):
+            if r < SHIFT:
+                part, beyond = both[r + SHIFT, near], both_r[r]
+            else:
+                part, beyond = both_b[r - SHIFT, near], both_d[r - SHIFT]
+            wide = part.astype(F32)
+            if b == steps - 1:
+                wide = jnp.concatenate([wide, beyond.astype(F32)], 0)
+            wide = wide[SHIFT : SHIFT + span_cols]
+            unit[win_at, r] = wide[:, 0:C].reshape(step_wins, WIN, C)
+            gradf[win_at, r] = wide[:, C : 2 * C].reshape(step_wins, WIN, C)
 
         x = unit[win_at].reshape(step, C)
         center = jnp.mean(x, -1, keepdims=True)
@@ -272,12 +266,15 @@
             g - jnp.mean(g, -1, keepdims=True) - x * jnp.mean(g * x, -1, keepdims=True)
         )
         out = (gradf[win_at].reshape(step, C) + dx).reshape(step_wins, WIN, WIN, C)
-        for r in range(WIN):
+        for r in range(SHIFT):
             frame_low[r, cols] = out[:, r].reshape(span_cols, C).astype(BF16)
-        back(frame_low.at[SHIFT:WIN, cols], back_u.at[0:SHIFT, cols], down, col)
+        for r in range(0, SHIFT, 2):
+            two = [out[:, SHIFT + r + i].reshape(span_cols, C) for i in range(2)]
+            frame_two[r // 2, cols] = jnp.concatenate(two, 1).astype(BF16)
+        back(frame_two.at[0:2, cols], back_u.at[0:2, cols], down, col)
         if b == steps - 1:
             back(frame_low.at[0:SHIFT, edge:tile_cols], back_l, row, other)
-            back(frame_low.at[SHIFT:WIN, edge:tile_cols], back_ul, down, other)
+            back(frame_two.at[0:2, edge:tile_cols], back_ul, down, other)
 
     for i, part in enumerate((dq_s, dk_s, dv_s)):
         pack[i * BLOCK : (i + 1) * BLOCK, 0:C] = mul(nt_s[...], part[...])[0:BLOCK]
@@ -319,7 +316,9 @@
         copy.wait()
     for r in range(WIN):
         if r < SHIFT:
-            left_part, main_part = back_ul[r], back_u[r]
+            lanes = slice((r % 2) * C, (r % 2 + 1) * C)
+            left_part = back_ul[r // 2].astype(F32)[:, lanes]
+            main_part = back_u[r // 2].astype(F32)[:, lanes]
         else:
             left_part, main_part = back_l[r - SHIFT], frame_low[r - SHIFT]
         wide = jnp.concatenate([left_part.astype(F32), main_part.astype(F32)], 0)
@@ -391,9 +390,16 @@
     total_tokens = tokens.shape[0] * tile_cols * rows_n * cols_n
     vmem = pltpu.VMEM
     halo = [
+        vmem((SHIFT, tile_cols, 2 * C), BF16),
+        vmem((SHIFT, EDGE, 2 * C), BF16),
+        vmem((SHIFT, EDGE, 2 * C), BF16),
+    ]
+    home = [
         vmem((SHIFT, tile_cols, C), BF16),
+        vmem((2, tile_cols, 2 * C), BF16),
+        vmem((2, tile_cols, 2 * C), BF16),
         vmem((SHIFT, EDGE, C), BF16),
-        vmem((SHIFT, EDGE, C), BF16),
+        vmem((2, EDGE, 2 * C), BF16),
     ]
     flat_low = vmem((count, C), BF16)
     whole = pl.BlockSpec(memory_space=pltpu.VMEM)
@@ -409,9 +415,9 @@
             jax.ShapeDtypeStruct((1, C), F32),
             jax.ShapeDtypeStruct((1, C), F32),
         ),
-        in_specs=[whole] * 9,
+        in_specs=[whole] * 8,
         out_specs=(whole,) * 7,
-        scratch_shapes=halo + halo + [
+        scratch_shapes=halo + [
             vmem(regions.shape, jnp.int32),
             vmem(regions.shape, jnp.int32),
             vmem((wins, WIN, WIN, C), F32),
@@ -430,15 +436,14 @@
             vmem((SPAN, LANES), F32),
             vmem((WIN * SPAN, 128), BF16),
             vmem((WIN * 128, 256), BF16),
-            vmem((WIN, tile_cols, C), BF16),
-        ] + halo + [
+        ] + home + [
             vmem((rows_total, 256), F32),
             vmem((rows_total, 256), BF16),
             vmem((half, 256), BF16),
             vmem((half, 256), BF16),
             vmem((rows_n, chunk, 256), BF16),
             vmem((2, half, 256), BF16),
-            dma((6 + 2 * steps,)), dma((6 + 2 * steps,)),
+            dma((4 + steps,)), dma((4 + steps,)),
             dma((steps + 2,)), dma((steps + 2,)), dma((2,)),
             dma((rows_n,)), dma((rows_n,)), dma((rows_n,)), dma((rows_n,)),
             dma((rows_n,)), dma((rows_n,)),
@@ -447,7 +452,7 @@
             collective_id=0, has_side_effects=True, vmem_limit_bytes=48 * 1024 * 1024
         ),
     )(
-        tokens, grad_out, regions, ln_gain.reshape(1, C), ln_offset.reshape(1, C), qkv_weight,
+        jnp.concatenate([tokens, grad_out], -1), regions, ln_gain.reshape(1, C), ln_offset.reshape(1, C), qkv_weight,
         qkv_bias.reshape(1, 3 * C), proj_weight, bias_table.T,
     )
     d_tokens, d_qkvw, d_qkvb, d_projw, d_table, d_gain, d_offset = outs

time: 53.6 us -> 52.4 us (0.978)
  Pallas kernels: 44.9 us -> 43.5 us
    pallas_call x1, Pallas kernels: 44.9 us -> 43.5 us  [on_device(): pl.pallas_call(functools.partial(body, rows_n, cols_n, rows_total, total_...]
    reshape x1, local copies, waits for them, and re-layouts: 0.01 us -> 0.74 us  [on_device(): qkv_bias.reshape(1, 3 * C)]
    unnamed x24 -> x22, local copies, waits for them, and re-layouts: 7.11 us -> 6.38 us
where the time goes in v4:
time: 52.4 us; the launch traced here: 52.2 us
  Pallas kernels  43.5 us (83%)
  local copies, waits for them, and re-layouts  7.11 us (14%)
  other arithmetic  0.91 us (2%)
  between operations  0.73 us (1%)
    pallas_call x1, Pallas kernels, on_device(): pl.pallas_call(functools.partial(body, rows_n, cols_n, rows_total, total_...  43.5 us
    unnamed x22, local copies, waits for them, and re-layouts  6.38 us

profile of v4, /device:TPU:0, one launch (start us, length us, event | category | flops | bytes accessed | tf_op | source)
XLA Modules:
  0.0 52.2 jit_solution(10294121952461330066)
XLA Ops:
  0.6 0.0 copy-start.6
  0.6 0.7 %reshape.34.qkvb = f32[1,540]{1,0:T(1,128)S(1)} reshape(f32[540]{0:T(1024)} %param.15) | data formatting | bytes 4320 | tf_op jit(solution)/shard_map/reshape | solution.py:456
  1.4 1.2 %copy.16 = bf16[8,128,180]{2,1,0:T(8,128)(2,1)S(1)} copy(bf16[8,128,180]{1,0,2:T(8,128)(2,1)} %param.9) | data formatting | bytes 737280 | tf_op args[0]
  2.6 0.0 copy-done.6
  2.6 0.3 copy.17
  2.9 0.0 copy-start
  3.0 0.0 copy-start.1
  3.0 0.0 copy-start.2
  3.0 0.0 copy-start.3
  3.0 0.0 copy-start.4
  3.0 0.0 copy-start.5
  3.0 0.3 pad_maximum_fusion.both
  3.3 0.6 %copy-done = bf16[180,540]{1,0:T(8,128)(2,1)S(1)} copy-done((bf16[180,540]{1,0:T(8,128)(2,1)S(1)}, bf16[180,540]{1,0:T(8,128)(2,1)}, u32[]{:S(2)}) %copy-start) | copy-done | bytes 194424
  3.9 0.1 copy-done.1
  4.0 0.0 copy-done.2
  4.0 0.0 copy-done.3
  4.0 0.0 copy-done.4
  4.0 0.0 copy-done.5
  4.0 43.5 %shard_map.144 = (bf16[8,128,180]{2,1,0:T(8,128)(2,1)S(1)}, f32[180,540]{1,0:T(8,128)S(1)}, f32[1,540]{1,0:T(1,128)S(1)}, f32[180,180]{1,0:T(8,128)S(1)}, f32[6,...) custom-call(bf16[8,128,360]{2,1,0:T(8,128)(2,1)S(1)} %pad_maximum_fusion.both, s32[8,128]{1,0:T(8,128)S(1)} %copy-done.3, ...), custom_call_target="tpu_custom_call" | custom-call | tf_op jit(solution)/shard_map/pallas_call | solution.py:407
  47.4 1.0 %copy.18 = bf16[8,128,180]{1,0,2:T(8,128)(2,1)} copy(bf16[8,128,180]{2,1,0:T(8,128)(2,1)S(1)} %get-tuple-element.21) | data formatting | bytes 737280
  48.4 0.6 %reduce = f32[540]{0:T(1024)} reduce(f32[1,540]{1,0:T(1,128)S(1)} %get-tuple-element.16, f32[]{:T(128)} %constant.3), dimensions={0}, to_apply=%get-tuple-element.16.reduce_sub_computation | reduce | bytes 4324 | tf_op jit(solution)/shard_map/pallas_call | solution.py:407
  49.0 0.8 %copy.24 = f32[180,540]{1,0:T(8,128)} copy(f32[180,540]{1,0:T(8,128)S(1)} %get-tuple-element.36) | data formatting | bytes 777600
  49.8 0.7 %copy.25 = f32[180,180]{1,0:T(8,128)} copy(f32[180,180]{1,0:T(8,128)S(1)} %get-tuple-element.38) | data formatting | bytes 259200
  50.5 0.6 %copy.26 = f32[225,6]{0,1:T(8,128)} copy(f32[225,6]{0,1:T(8,128)S(1)} %bitcast.7) | data formatting | bytes 10800
  51.1 0.6 %copy.27 = f32[180]{0:T(256)} copy(f32[180]{0:T(256)S(1)} %bitcast.9) | data formatting | bytes 1440
  51.7 0.6 %copy.28 = f32[180]{0:T(256)} copy(f32[180]{0:T(256)S(1)} %bitcast.8) | data formatting | bytes 1440
Async XLA Ops:
  0.6 2.0 %copy-start.6 = (bf16[8,128,180]{1,0,2:T(8,128)(2,1)S(1)}, bf16[8,128,180]{1,0,2:T(8,128)(2,1)}, u32[]{:S(2)}) copy-start(bf16[8,128,180]{1,0,2:T(8,128)(2,1)} %param.10) | copy-start | bytes 1105924
  2.9 0.9 %copy-start = (bf16[180,540]{1,0:T(8,128)(2,1)S(1)}, bf16[180,540]{1,0:T(8,128)(2,1)}, u32[]{:S(2)}) copy-start(bf16[180,540]{1,0:T(8,128)(2,1)} %qkvw.1) | copy-start | bytes 583204
  3.0 1.0 %copy-start.1 = (bf16[180,180]{1,0:T(8,128)(2,1)S(1)}, bf16[180,180]{1,0:T(8,128)(2,1)}, u32[]{:S(2)}) copy-start(bf16[180,180]{1,0:T(8,128)(2,1)} %projw.1) | copy-start | bytes 194404
  3.0 1.0 %copy-start.2 = (f32[225,6]{0,1:T(8,128)S(1)}, f32[225,6]{0,1:T(8,128)}, u32[]{:S(2)}) copy-start(f32[225,6]{0,1:T(8,128)} %param.17) | copy-start | bytes 16204
  3.0 1.0 %copy-start.3 = (s32[8,128]{1,0:T(8,128)S(1)}, s32[8,128]{1,0:T(8,128)}, u32[]{:S(2)}) copy-start(s32[8,128]{1,0:T(8,128)} %reg.1) | copy-start | bytes 12292
  3.0 1.0 %copy-start.4 = (f32[180]{0:T(256)S(1)}, f32[180]{0:T(256)}, u32[]{:S(2)}) copy-start(f32[180]{0:T(256)} %param.12) | copy-start | bytes 2164
  3.0 1.0 %copy-start.5 = (f32[180]{0:T(256)S(1)}, f32[180]{0:T(256)}, u32[]{:S(2)}) copy-start(f32[180]{0:T(256)} %param.13) | copy-start | bytes 2164
